TPU v7x, 32 devices: a whole 2x2x4 slice. The times are simulated.
32 devices in a mesh: light: 2 (over y), view: 16 (over z, x, core).
Axes of the slice: x: 2, y: 2, z: 4, core: 2. Of those that a mesh axis runs over, the one named last changes fastest.
Arguments:
- density: bfloat16 [8, 256, 2048], P('light', 'view'), may hold values from 0 to 1
- occupied: int32 [2, 16, 16], P('light', 'view'), may hold values from 0 to 1, as said below
- view_sign: float32 [1], replicated, may hold values from -1 to 1, as said below
- transfer: float32 [4, 4], replicated, may hold values from -3 to 3
- absorb: float32 [3], replicated, may hold values from 0.5 to 20
- light_in: float32 [3, 256, 2048], P(None, 'view'), may hold values from 1 to 2.5
Outputs:
- image: float32 [4, 16384], P(None, ('light', 'view'))
Inputs may be any that keep to these rules, and one draw needn't show every extreme that they name: `occupied`: 0 or 1; the share of occupied bricks differs from device to device. `view_sign`: magnitude 0.5 or more; either sign.
All inputs are finite; a program needn't handle non-finite values.
Results may differ from a plain program's by a relative error of at most 0.0003.
Values may be sent and summed in bfloat16 or wider, within the bound.
A program may use at most 64 MiB of HBM per device.

v0:
```python
import jax
import jax.numpy as jnp
from jax import lax
from jax.sharding import PartitionSpec as P


def with_halo(cells, sides, width):
    for axis, dim in sides:
        count = lax.axis_size(axis)
        ends = count - 1
        head = lax.slice_in_dim(cells, 0, width, axis=dim)
        tail = lax.slice_in_dim(cells, cells.shape[dim] - width, cells.shape[dim], axis=dim)
        cells = jnp.concatenate(
            [
                lax.ppermute(tail, axis, [(i, (i + 1) % count) for i in range(ends)]),
                cells,
                lax.ppermute(head, axis, [((i + 1) % count, i) for i in range(ends)]),
            ],
            axis=dim,
        )
    return cells


def from_behind(x, axis, by):
    length = lax.axis_size(axis)
    pairs = [(i, i + by) for i in range(length) if 0 <= i + by < length]
    return lax.ppermute(x, axis, pairs)


def polynomial(coeffs, values):
    return coeffs[0] + values * (coeffs[1] + values * (coeffs[2] + values * coeffs[3]))


def blur_columns(field):
    widths = [(0, 0)] * (field.ndim - 1) + [(1, 1)]
    padded = jnp.pad(field, widths)
    return 0.25 * padded[..., :-2] + 0.5 * padded[..., 1:-1] + 0.25 * padded[..., 2:]


def composite_depth(emitted, opacity, facing_back):
    emitted = jnp.where(facing_back == 1, jnp.flip(emitted, 1), emitted)
    opacity = jnp.where(facing_back == 1, jnp.flip(opacity, 0), opacity)
    passing = 1.0 - opacity
    through = jnp.cumprod(passing, axis=0)
    before = jnp.concatenate([jnp.ones_like(passing[:1]), through[:-1]], axis=0)
    colour = jnp.sum(before[None] * emitted, axis=1)
    return jnp.concatenate([colour, (1.0 - through[-1])[None]], axis=0)


def propagate(light_front, transmit):

    def advance(carried, factor):
        return (blur_columns(carried * factor), None)

    result, _ = lax.scan(advance, light_front, transmit)
    return result


def body(density, occupied, view_sign, transfer, absorb, light_in):
    cells_x, cells_y, columns = density.shape
    light_count = lax.axis_size("light")
    view_count = lax.axis_size("view")
    total_x = cells_x * light_count
    total_y = cells_y * view_count
    light_pos = lax.axis_index("light")
    facing_back = (view_sign[0] < 0.0).astype(jnp.int32)
    path_length = 2.0 / total_y / jnp.abs(view_sign[0])
    padded = with_halo(density, (("light", 0),), 1).astype(jnp.float32)
    centre = padded[1:-1, :, :]
    grad_x = 0.5 * (padded[2:, :, :] - padded[:-2, :, :])
    side_y = jnp.pad(centre, ((0, 0), (1, 1), (0, 0)), mode="edge")
    grad_y = 0.5 * (side_y[:, 2:, :] - side_y[:, :-2, :])
    side_z = jnp.pad(centre, ((0, 0), (0, 0), (1, 1)))
    grad_z = 0.5 * (side_z[:, :, 2:] - side_z[:, :, :-2])
    bricks = occupied.shape[2]
    occupancy = jnp.broadcast_to(
        occupied[0, 0].astype(jnp.float32)[:, None], (bricks, columns // bricks)
    ).reshape(columns)
    extinction = jax.nn.softplus(polynomial(transfer[0], centre)) * occupancy
    opacity = 1.0 - jnp.exp(-extinction * path_length)
    colour = jnp.stack(
        [jax.nn.sigmoid(polynomial(transfer[channel], centre)) for channel in (1, 2, 3)], axis=1
    )
    facing = (0.8 * grad_x + 0.36 * grad_y + 0.48 * grad_z) * lax.rsqrt(
        1.0 + grad_x * grad_x + grad_y * grad_y + grad_z * grad_z
    )
    shading = 0.65 + 0.35 * facing
    transmit = jnp.exp(-absorb[None, :, None, None] * extinction[:, None] / total_x)
    incoming = light_in
    for turn_index in range(light_count - 1):
        outgoing = propagate(incoming, transmit)
        arrived = from_behind(outgoing.astype(jnp.bfloat16), "light", 1).astype(outgoing.dtype)
        incoming = jnp.where(light_pos == 0, light_in, arrived)

    def shade_layer(light_front, layer):
        layer_opacity, layer_colour, layer_shading, layer_transmit = layer
        emitted = layer_opacity[None] * layer_colour * (0.2 + light_front * layer_shading[None])
        pixel_row = composite_depth(emitted, layer_opacity, facing_back)
        return (blur_columns(light_front * layer_transmit), pixel_row)

    _, pixel_rows = lax.scan(shade_layer, incoming, (opacity, colour, shading, transmit))
    partial_image = jnp.transpose(pixel_rows, (1, 0, 2)).reshape(4, cells_x * columns)
    piece_len = cells_x * columns // view_count
    blocks = partial_image.reshape(4, view_count, piece_len)
    received = lax.all_to_all(blocks, "view", split_axis=1, concat_axis=1, tiled=True)
    ordered = jnp.where(facing_back == 1, jnp.flip(received, 1), received)
    passing = 1.0 - ordered[3]
    through = jnp.cumprod(passing, axis=0)
    before = jnp.concatenate([jnp.ones_like(passing[:1]), through[:-1]], axis=0)
    return jnp.sum(before[None] * ordered, axis=1)


def solution(mesh):
    in_specs = (
        P("light", "view", None),
        P("light", "view", None),
        P(),
        P(),
        P(),
        P(None, "view", None),
    )
    out_specs = P(None, ("light", "view"))
    return jax.shard_map(body, mesh=mesh, in_specs=in_specs, out_specs=out_specs, check_vma=False)
```

profile of v0, /device:TPU:0, one launch (start us, length us, event | category | flops | bytes accessed | tf_op | source)
XLA Modules:
  0.0 64.3 jit_solution(16687170693016791950)
XLA Ops:
  0.0 0.9 %fusion.14 = (bf16[1,16,2048]{2,1,0:T(8,128)(2,1)S(1)}, bf16[1,16,2048]{2,1,0:T(8,128)(2,1)S(1)}) fusion(bf16[4,16,2048]{2,1,0:T(8,128)(2,1)} %param.10), kind=kLoop, calls=%fused_computation.49 | loop fusion | bytes 262144 | tf_op jit(solution)/shard_map/slice | solution.py:12
  0.9 4.9 %collective-permute-start = (bf16[1,16,2048]{2,1,0:T(8,128)(2,1)S(1)}, bf16[1,16,2048]{2,1,0:T(8,128)(2,1)S(1)}, u32[]{:S(2)}, u32[]{:S(2)}) collective-permute-start(bf16[1,16,2048]{2,1,0:T(8,128)(2,1)S(1)} %get-tuple-element.210), channel_id=1, source_target_pairs={{0,16},{1,17},{2,18},{3,19},{4,20},{5,21},{6,22},{7,23},{8,24},{9,... | collective-permute-start | bytes 196616 | tf_op jit(solution)/shard_map/ppermute | solution.py:15
  5.8 1.3 %collective-permute-start.1 = (bf16[1,16,2048]{2,1,0:T(8,128)(2,1)S(1)}, bf16[1,16,2048]{2,1,0:T(8,128)(2,1)S(1)}, u32[]{:S(2)}, u32[]{:S(2)}) collective-permute-start(bf16[1,16,2048]{2,1,0:T(8,128)(2,1)S(1)} %get-tuple-element.211), channel_id=1, source_target_pairs={{16,0},{17,1},{18,2},{19,3},{20,4},{21,5},{22,6},{23,7},{24,8},{25... | collective-permute-start | bytes 196616 | tf_op jit(solution)/shard_map/ppermute | solution.py:17
  7.7 0.7 %convert_bitcast_fusion = f32[16]{0:T(128)S(1)} fusion(s32[1,1,16]{2,1,0:T(1,128)} %param.11), kind=kLoop, calls=%fused_computation.48 | loop fusion | flops 16 | bytes 128 | tf_op jit(solution)/shard_map/convert_element_type | solution.py:77
  8.4 0.1 broadcast_bitcast_fusion
  8.5 0.7 %neg.20 = f32[3]{0:T(128)S(1)} negate(f32[3]{0:T(128)} %param.14) | non-fusion elementwise | flops 3 | bytes 24 | tf_op jit(solution)/shard_map/neg | solution.py:88
  9.2 2.0 %fusion.15 = (f32[1,1]{1,0:T(1,128)}, f32[1,1]{1,0:T(1,128)}, f32[1,1]{1,0:T(1,128)}, f32[1,1]{1,0:T(1,128)}, f32[1,1]{1,0:T(1,128)}, /*index=5*/f32[1,1]{1,0:T(...) fusion(f32[4,4]{1,0:T(4,128)} %param.13), kind=kLoop, calls=%fused_computation.50 | loop fusion | bytes 128 | tf_op jit(solution)/shard_map/slice | solution.py:31
  11.1 0.0 collective-permute-done
  11.1 0.8 %collective-permute-done.1 = bf16[1,16,2048]{2,1,0:T(8,128)(2,1)S(1)} collective-permute-done((bf16[1,16,2048]{2,1,0:T(8,128)(2,1)S(1)}, bf16[1,16,2048]{2,1,0:T(8,128)(2,1)S(1)}, u32[]{:S(2)}, u32[]{:S(2)}) %collective-permute-start.1) | collective-permute-done | bytes 65568 | tf_op jit(solution)/shard_map/ppermute | solution.py:17
  11.9 1.0 %maximum_convert_fusion = f32[6,16,2048]{2,1,0:T(8,128)S(1)} fusion(bf16[1,16,2048]{2,1,0:T(8,128)(2,1)S(1)} %collective-permute-done.1, bf16[4,16,2048]{2,1,0:T(8,128)(2,1)} %param.10, bf16[1,16,2048]{2,1,0:T(8,128)(2,1)S(1)} %collective-permute-done), kind=kLoop, calls=%fused_computation.39 | loop fusion | flops 589824 | bytes 1179648 | tf_op jit(solution)/shard_map/convert_element_type | solution.py:68
  12.9 6.7 %exponential_subtract_fusion = (f32[4,16,2048]{2,1,0:T(8,128)}, f32[4,16,2048]{2,1,0:T(8,128)S(1)}, f32[4,16,2048]{2,1,0:T(8,128)}, f32[4,1,16,2048]{3,2,0,1:T(8,128)S(1)}) fusion(f32[]{:T(128)} %bitcast.13, f32[2048]{0:T(1024)S(1)} %broadcast_bitcast_fusion, f32[]{:T(128)} %bitcast.10, f32[]{:T(128)} %bitcast.9, f32[]{:T(128)} %bitcast.8, ...), kind=kLoop, calls=%fused_computation.38 | loop fusion | flops 3276800 | bytes 2629668 | tf_op jit(solution)/shard_map/sub | solution.py:80
  19.6 0.0 copy-start.1
  19.6 0.3 multiply_exponential_fusion
  19.9 0.7 %copy-done.1 = f32[3,16,2048]{2,1,0:T(8,128)S(1)} copy-done((f32[3,16,2048]{2,1,0:T(8,128)S(1)}, f32[3,16,2048]{2,1,0:T(8,128)}, u32[]{:S(2)}) %copy-start.1) | copy-done | bytes 393240
  20.6 1.3 %while.26 = (s32[]{:T(128)}, f32[3,16,2048]{2,1,0:T(8,128)S(1)}, f32[4,3,16,2048]{3,2,1,0:T(8,128)S(1)}, s32[]{:T(128)}) while((s32[]{:T(128)}, f32[3,16,2048]{2,1,0:T(8,128)S(1)}, f32[4,3,16,2048]{3,2,1,0:T(8,128)S(1)}, s32[]{:T(128)}) %tuple.85), condition=%wide.region_1.2_spmd, body=%wide.region_0.1_spmd.sunk | while | flops 589826 | bytes 1966137 | solution.py:55
  20.6 0.3 fusion.20
  21.0 0.3 fusion.20
  21.3 0.3 fusion.20
  21.7 0.3 fusion.20
  22.0 3.8 %collective-permute-start.2 = (bf16[3,16,2048]{2,1,0:T(8,128)(2,1)S(1)}, bf16[3,16,2048]{2,1,0:T(8,128)(2,1)S(1)}, u32[]{:S(2)}, u32[]{:S(2)}) collective-permute-start(bf16[3,16,2048]{2,1,0:T(8,128)(2,1)S(1)} %convert_element_type.36), channel_id=1, source_target_pairs={{0,16},{1,17},{2,18},{3,19},{4,20},{5,21},{6,22},{7,23},{8,24},{9,... | collective-permute-start | bytes 589832 | tf_op jit(solution)/shard_map/ppermute | solution.py:27
  25.8 1.0 %maximum_convert_fusion.2 = (f32[4,1,2048]{2,1,0:T(1,128)S(1)}, f32[4,1,2048]{2,1,0:T(1,128)S(1)}) fusion(bf16[1,16,2048]{2,1,0:T(8,128)(2,1)S(1)} %collective-permute-done.1, bf16[4,16,2048]{2,1,0:T(8,128)(2,1)} %param.10, bf16[1,16,2048]{2,1,0:T(8,128)(2,1)S(1)} %collective-permute-done), kind=kLoop, calls=%fused_computation.45 | loop fusion | flops 98304 | bytes 458752 | tf_op jit(solution)/shard_map/jit(_pad)/slice | solution.py:71
  26.8 8.4 %multiply_add_fusion = (f32[4,16,2048]{2,1,0:T(8,128)}, f32[4,1,16,2048]{3,2,0,1:T(8,128)S(1)}, f32[4,1,16,2048]{3,2,0,1:T(8,128)S(1)}) fusion(f32[4,16,2048]{2,1,0:T(8,128)} %get-tuple-element.206, f32[4,1,2048]{2,1,0:T(1,128)S(1)} %get-tuple-element.209, f32[4,1,2048]{2,1,0:T(1,128)S(1)} %get-tuple-element.208, f32[6,16,2048]{2,1,0:T(8,128)S(1)} %maximum_convert_fusion, ...), kind=kLoop, calls=%fused_computation.34 | loop fusion | flops 5242880 | bytes 3735584 | tf_op jit(solution)/shard_map/add | solution.py:87
  35.2 0.0 copy-start
  35.2 1.3 %pad_maximum_fusion = f32[4,3,16,2048]{3,2,0,1:T(8,128)} fusion(f32[4,1,16,2048]{3,2,0,1:T(8,128)S(1)} %get-tuple-element.205, f32[4,1,16,2048]{3,2,0,1:T(8,128)S(1)} %get-tuple-element.207, f32[4,1,16,2048]{3,2,0,1:T(8,128)S(1)} %get-tuple-element.204), kind=kLoop, calls=%fused_computation.23 | loop fusion | flops 786432 | bytes 3145728 | tf_op jit(solution)/shard_map/stack | solution.py:81
  36.4 0.0 collective-permute-done.2
  36.4 0.0 copy-done
  36.5 13.4 %while.27 = (s32[]{:T(128)}, f32[3,16,2048]{2,1,0:T(8,128)S(1)}, f32[4,4,2048]{2,1,0:T(4,128)S(1)}, f32[4,3,16,2048]{3,2,1,0:T(8,128)S(1)}, pred[]{:T(512)}, /*i...) while((s32[]{:T(128)}, f32[3,16,2048]{2,1,0:T(8,128)S(1)}, ...), condition=%wide.region_5.6_spmd, body=%wide.region_2.5_spmd.sunk | while | flops 1839106 | bytes 6529147 | solution.py:101
  36.5 1.0 %dynamic-slice_bitcast_fusion.3 = (f32[16,2048]{1,0:T(8,128)S(1)}, f32[16,2048]{1,0:T(8,128)S(1)}) fusion(f32[4,16,2048]{2,1,0:T(8,128)} %get-tuple-element.343, s32[]{:T(128)} %get-tuple-element.326, f32[4,16,2048]{2,1,0:T(8,128)} %get-tuple-element.341), kind=kLoop, calls=%fused_computation.17.clone.1 | loop fusion | bytes 524292 | tf_op jit(solution)/shard_map/while/body/eval_jaxpr/mul | solution.py:97
  37.5 1.1 %fusion.21 = (f32[3,16,2048]{2,1,0:T(8,128)S(1)}, f32[3,16,2048]{2,1,0:T(8,128)S(1)}) fusion(f32[3,16,2048]{2,1,0:T(8,128)S(1)} %get-tuple-element.327, f32[4,3,16,2048]{3,2,0,1:T(8,128)} %get-tuple-element.342, s32[]{:T(128)} %get-tuple-element.326, f32[16,2048]{1,0:T(8,128)S(1)} %get-tuple-element.300, f32[16,2048]{1,0:T(8,128)S(1)} %get-tuple-element.301, ...), kind=kLoop, calls=%fused_computation.14.clone.1 | loop fusion | flops 491520 | bytes 2228228 | tf_op jit(solution)/shard_map/while/body/eval_jaxpr/mul | solution.py:97
  38.6 0.3 rev.25
  38.9 0.3 rev.24
  39.3 0.1 reduce_window.23
  39.4 0.1 multiply_reduce_fusion.3
  39.6 0.3 fusion.22
  39.8 1.0 %dynamic-slice_bitcast_fusion.3 = (f32[16,2048]{1,0:T(8,128)S(1)}, f32[16,2048]{1,0:T(8,128)S(1)}) fusion(f32[4,16,2048]{2,1,0:T(8,128)} %get-tuple-element.343, s32[]{:T(128)} %get-tuple-element.326, f32[4,16,2048]{2,1,0:T(8,128)} %get-tuple-element.341), kind=kLoop, calls=%fused_computation.17.clone.1 | loop fusion | bytes 524292 | tf_op jit(solution)/shard_map/while/body/eval_jaxpr/mul | solution.py:97
  40.8 1.1 %fusion.21 = (f32[3,16,2048]{2,1,0:T(8,128)S(1)}, f32[3,16,2048]{2,1,0:T(8,128)S(1)}) fusion(f32[3,16,2048]{2,1,0:T(8,128)S(1)} %get-tuple-element.327, f32[4,3,16,2048]{3,2,0,1:T(8,128)} %get-tuple-element.342, s32[]{:T(128)} %get-tuple-element.326, f32[16,2048]{1,0:T(8,128)S(1)} %get-tuple-element.300, f32[16,2048]{1,0:T(8,128)S(1)} %get-tuple-element.301, ...), kind=kLoop, calls=%fused_computation.14.clone.1 | loop fusion | flops 491520 | bytes 2228228 | tf_op jit(solution)/shard_map/while/body/eval_jaxpr/mul | solution.py:97
  41.9 0.3 rev.25
  42.3 0.3 rev.24
  42.6 0.1 reduce_window.23
  42.7 0.1 multiply_reduce_fusion.3
  42.9 0.3 fusion.22
  43.2 1.0 %dynamic-slice_bitcast_fusion.3 = (f32[16,2048]{1,0:T(8,128)S(1)}, f32[16,2048]{1,0:T(8,128)S(1)}) fusion(f32[4,16,2048]{2,1,0:T(8,128)} %get-tuple-element.343, s32[]{:T(128)} %get-tuple-element.326, f32[4,16,2048]{2,1,0:T(8,128)} %get-tuple-element.341), kind=kLoop, calls=%fused_computation.17.clone.1 | loop fusion | bytes 524292 | tf_op jit(solution)/shard_map/while/body/eval_jaxpr/mul | solution.py:97
  44.2 1.1 %fusion.21 = (f32[3,16,2048]{2,1,0:T(8,128)S(1)}, f32[3,16,2048]{2,1,0:T(8,128)S(1)}) fusion(f32[3,16,2048]{2,1,0:T(8,128)S(1)} %get-tuple-element.327, f32[4,3,16,2048]{3,2,0,1:T(8,128)} %get-tuple-element.342, s32[]{:T(128)} %get-tuple-element.326, f32[16,2048]{1,0:T(8,128)S(1)} %get-tuple-element.300, f32[16,2048]{1,0:T(8,128)S(1)} %get-tuple-element.301, ...), kind=kLoop, calls=%fused_computation.14.clone.1 | loop fusion | flops 491520 | bytes 2228228 | tf_op jit(solution)/shard_map/while/body/eval_jaxpr/mul | solution.py:97
  45.3 0.3 rev.25
  45.6 0.3 rev.24
  45.9 0.1 reduce_window.23
  46.1 0.1 multiply_reduce_fusion.3
  46.3 0.3 fusion.22
  46.5 1.0 %dynamic-slice_bitcast_fusion.3 = (f32[16,2048]{1,0:T(8,128)S(1)}, f32[16,2048]{1,0:T(8,128)S(1)}) fusion(f32[4,16,2048]{2,1,0:T(8,128)} %get-tuple-element.343, s32[]{:T(128)} %get-tuple-element.326, f32[4,16,2048]{2,1,0:T(8,128)} %get-tuple-element.341), kind=kLoop, calls=%fused_computation.17.clone.1 | loop fusion | bytes 524292 | tf_op jit(solution)/shard_map/while/body/eval_jaxpr/mul | solution.py:97
  47.5 1.1 %fusion.21 = (f32[3,16,2048]{2,1,0:T(8,128)S(1)}, f32[3,16,2048]{2,1,0:T(8,128)S(1)}) fusion(f32[3,16,2048]{2,1,0:T(8,128)S(1)} %get-tuple-element.327, f32[4,3,16,2048]{3,2,0,1:T(8,128)} %get-tuple-element.342, s32[]{:T(128)} %get-tuple-element.326, f32[16,2048]{1,0:T(8,128)S(1)} %get-tuple-element.300, f32[16,2048]{1,0:T(8,128)S(1)} %get-tuple-element.301, ...), kind=kLoop, calls=%fused_computation.14.clone.1 | loop fusion | flops 491520 | bytes 2228228 | tf_op jit(solution)/shard_map/while/body/eval_jaxpr/mul | solution.py:97
  48.6 0.3 rev.25
  49.0 0.3 rev.24
  49.3 0.1 reduce_window.23
  49.4 0.1 multiply_reduce_fusion.3
  49.6 0.3 fusion.22
  49.9 13.6 %all_to_all.5 = f32[4,16,512]{2,0,1:T(4,128)S(1)} all-to-all(f32[4,16,512]{2,0,1:T(4,128)S(1)} %bitcast.65), channel_id=1, replica_groups=mesh['light'=2,'view'=16] {'view'}, dimensions={1} | all-to-all | bytes 262144 | tf_op jit(solution)/shard_map/all_to_all | solution.py:105
  63.7 0.7 %multiply_reduce_fusion.1 = f32[4,512]{1,0:T(4,128)} fusion(f32[16,512]{1,0:T(8,128)S(1)} %concatenate.26, f32[4,16,512]{2,0,1:T(4,128)S(1)} %all_to_all.5, pred[]{:T(512)} %bitcast.6), kind=kLoop, calls=%fused_computation.42 | loop fusion | flops 96256 | bytes 172033 | tf_op jit(solution)/shard_map/reduce_sum | solution.py:110
  (28 shorter events, 0.7 us)
Async XLA Ops:
  0.9 10.3 %collective-permute-start = (bf16[1,16,2048]{2,1,0:T(8,128)(2,1)S(1)}, bf16[1,16,2048]{2,1,0:T(8,128)(2,1)S(1)}, u32[]{:S(2)}, u32[]{:S(2)}) collective-permute-start(bf16[1,16,2048]{2,1,0:T(8,128)(2,1)S(1)} %get-tuple-element.210), channel_id=1, source_target_pairs={{0,16},{1,17},{2,18},{3,19},{4,20},{5,21},{6,22},{7,23},{8,24},{9,... | collective-permute-start | bytes 196616 | tf_op jit(solution)/shard_map/ppermute | solution.py:15
  5.8 6.2 %collective-permute-start.1 = (bf16[1,16,2048]{2,1,0:T(8,128)(2,1)S(1)}, bf16[1,16,2048]{2,1,0:T(8,128)(2,1)S(1)}, u32[]{:S(2)}, u32[]{:S(2)}) collective-permute-start(bf16[1,16,2048]{2,1,0:T(8,128)(2,1)S(1)} %get-tuple-element.211), channel_id=1, source_target_pairs={{16,0},{17,1},{18,2},{19,3},{20,4},{21,5},{22,6},{23,7},{24,8},{25... | collective-permute-start | bytes 196616 | tf_op jit(solution)/shard_map/ppermute | solution.py:17
  19.6 1.0 %copy-start.1 = (f32[3,16,2048]{2,1,0:T(8,128)S(1)}, f32[3,16,2048]{2,1,0:T(8,128)}, u32[]{:S(2)}) copy-start(f32[3,16,2048]{2,1,0:T(8,128)} %param.15) | copy-start | bytes 1179652
  22.0 14.5 %collective-permute-start.2 = (bf16[3,16,2048]{2,1,0:T(8,128)(2,1)S(1)}, bf16[3,16,2048]{2,1,0:T(8,128)(2,1)S(1)}, u32[]{:S(2)}, u32[]{:S(2)}) collective-permute-start(bf16[3,16,2048]{2,1,0:T(8,128)(2,1)S(1)} %convert_element_type.36), channel_id=1, source_target_pairs={{0,16},{1,17},{2,18},{3,19},{4,20},{5,21},{6,22},{7,23},{8,24},{9,... | collective-permute-start | bytes 589832 | tf_op jit(solution)/shard_map/ppermute | solution.py:27
  35.2 1.3 %copy-start = (f32[3,16,2048]{2,1,0:T(8,128)S(1)}, f32[3,16,2048]{2,1,0:T(8,128)}, u32[]{:S(2)}) copy-start(f32[3,16,2048]{2,1,0:T(8,128)} %param.15) | copy-start | bytes 1179652
where the time goes:
time: 65.2 us; the launch traced here: 64.3 us
  other arithmetic  28.6 us (44%)
  blocking collectives  13.6 us (21%)
  local copies, waits for them, and re-layouts  10.2 us (16%)
  starting transfers between devices  9.96 us (15%)
  between operations  0.81 us (1%)
  waiting for transfers between devices  0.78 us (1%)
    all_to_all x1, blocking collectives, body(): lax.all_to_all(blocks, 'view', split_axis=1, concat_axis=1, tiled=True)  13.6 us
    add x1, other arithmetic, body(): shading = 0.65 + 0.35 * facing  8.35 us
    sub x1, other arithmetic, body(): opacity = 1.0 - jnp.exp(-extinction * path_length)  6.65 us
    ppermute x1, starting transfers between devices, with_halo(): lax.ppermute(tail, axis, [(i, (i + 1) % count) for i in range(ends)])  4.87 us
    mul x4, other arithmetic, shade_layer(): layer_opacity[None] * layer_colour  4.37 us
    mul x4, local copies, waits for them, and re-layouts, shade_layer(): light_front * layer_shading[None]  3.96 us
    ppermute x1, starting transfers between devices, from_behind(): return lax.ppermute(x, axis, pairs)  3.79 us
    add x8, other arithmetic, blur_columns(): 0.25 * padded[..., :-2] + 0.5 * padded[..., 1:-1] + 0.25 * padded[..., 2:]  2.16 us
  transfers between devices with their start and end apart: 3, of which 1 were waited for; matrix products, arithmetic and copies ran while one was open for 22% of the time, Pallas kernels for 0%

commit v1 on v0

v1 whole, which is shorter than its diff:
```python
import functools

import jax
import jax.numpy as jnp
from jax import lax
from jax.experimental import pallas as pl
from jax.experimental.pallas import tpu as pltpu
from jax.sharding import PartitionSpec as P

LANES = 128
HALF = LANES // 2
LOG2E = 1.4426950408889634
MESH = pl.DeviceIdType.MESH


class Plan:
    def __init__(self, lights, views, cells_x, cells_y, columns, bricks):
        self.lights, self.views = lights, views
        self.cx, self.cy = cells_x, cells_y
        self.nx, self.ny = cells_x * lights, cells_y * views
        self.tiles = columns // LANES
        self.rows = self.tiles // lights
        self.win_tiles = self.rows + (2 if lights > 2 else 1)
        self.width = self.win_tiles * LANES
        self.piece_rows = cells_x * self.tiles // views
        self.groups = self.rows // self.piece_rows
        self.per_layer = self.tiles // self.piece_rows
        self.tiles_per_brick = self.tiles // bricks
        self.bricks = bricks

    def window(self, light):
        return jnp.clip(light * self.rows - 1, 0, self.tiles - self.win_tiles)


def cubic(coeffs, x):
    return coeffs[0] + x * (coeffs[1] + x * (coeffs[2] + x * coeffs[3]))


def recip(x):
    r = pltpu.reciprocal(x, approx=True)
    return r * (2.0 - x * r)


def kernel(
    plan,
    density,
    occupied,
    view_sign,
    transfer,
    absorb,
    light_in,
    out,
    wbuf,
    lbuf,
    occ,
    dens,
    slope_z,
    front,
    edge_front,
    edge_prod,
    image,
    recv,
    dsem,
    dsend,
    osem,
    osend,
    lsem,
    isend,
    rsem,
):
    lights, views, rows, cy = plan.lights, plan.views, plan.rows, plan.cy
    me_l = lax.axis_index("light")
    me_v = lax.axis_index("view")
    win = plan.window(me_l)
    off = me_l * rows - win
    slab_of_me = ((me_v * plan.piece_rows) % plan.tiles) // rows

    barrier = pltpu.get_barrier_semaphore()
    for k in range(1, lights):
        pl.semaphore_signal(
            barrier, inc=1, device_id={"light": (me_l + k) % lights, "view": me_v}, device_id_type=MESH
        )

    def greet(v, carry):
        @pl.when(jnp.logical_or(v != me_v, slab_of_me != me_l))
        def _():
            pl.semaphore_signal(
                barrier, inc=1, device_id={"light": slab_of_me, "view": v}, device_id_type=MESH
            )

        return carry

    lax.fori_loop(0, views, greet, 0)

    def columns_of(light):
        return pl.ds(pl.multiple_of(plan.window(light) * LANES, LANES), plan.width)

    for i in range(plan.cx):
        layer = me_l * plan.cx + i
        pltpu.make_async_copy(
            density.at[i, :, columns_of(me_l)], wbuf.at[layer], dsem.at[layer]
        ).start()
    light_copy = pltpu.make_async_copy(light_in.at[:, :, columns_of(me_l)], lbuf, lsem)
    light_copy.start()

    for k in range(plan.bricks):
        value = jnp.full((plan.tiles_per_brick, LANES), occupied[0, 0, k].astype(jnp.float32))
        occ[me_l, k * plan.tiles_per_brick : (k + 1) * plan.tiles_per_brick, :] = value

    @pl.when(slab_of_me == me_l)
    def _():
        pl.semaphore_wait(barrier, lights - 1 + views - 1)

    @pl.when(slab_of_me != me_l)
    def _():
        pl.semaphore_wait(barrier, lights - 1 + views)

    def occ_copy(k):
        return pltpu.make_async_remote_copy(
            src_ref=occ.at[me_l],
            dst_ref=occ.at[me_l],
            send_sem=osend.at[k],
            recv_sem=osem.at[me_l],
            device_id={"light": (me_l + k) % lights, "view": me_v},
            device_id_type=MESH,
        )

    def dens_copy(k, i):
        other = (me_l + k) % lights
        layer = me_l * plan.cx + i
        return pltpu.make_async_remote_copy(
            src_ref=density.at[i, :, columns_of(other)],
            dst_ref=wbuf.at[layer],
            send_sem=dsend.at[k, i],
            recv_sem=dsem.at[layer],
            device_id={"light": other, "view": me_v},
            device_id_type=MESH,
        )

    for k in range(1, lights):
        occ_copy(k).start()
    for i in range(plan.cx):
        for k in range(1, lights):
            dens_copy(k, i).start()

    core = (rows, LANES)
    lane = lax.broadcasted_iota(jnp.int32, core, 1)
    sub = lax.broadcasted_iota(jnp.int32, core, 0)
    first_lane, last_lane = lane == 0, lane == LANES - 1
    first_row, last_row = sub == 0, sub == rows - 1
    flat = (cy, LANES)
    flat_lane = lax.broadcasted_iota(jnp.int32, flat, 1)
    flat_first, flat_last = flat_lane == 0, flat_lane == LANES - 1
    flat_low = flat_lane < HALF
    sign = jnp.full(core, view_sign[0])
    facing_back = sign < 0.0
    path_rate = (-2.0 * LOG2E / plan.ny) / jnp.abs(sign)
    rates = [absorb[c] * (-LOG2E / plan.nx) for c in range(3)]
    ext_coeffs = [transfer[0, k] * LOG2E for k in range(4)]
    colour_coeffs = [[transfer[c, k] * (-LOG2E) for k in range(4)] for c in (1, 2, 3)]
    has_left = jnp.where(me_l > 0, 1.0, 0.0)
    has_right = jnp.where(me_l < lights - 1, 1.0, 0.0)
    edge_tiles = [jnp.maximum(off - 1, 0)]
    if lights > 2:
        edge_tiles = [jnp.maximum(off - 1, 0), jnp.minimum(off + rows - 1, plan.win_tiles - 2)]
    else:
        edge_tiles = [jnp.where(me_l == 0, rows - 1, 0)]

    zeros = jnp.zeros((cy * rows, LANES), jnp.float32)
    dens[0] = zeros
    dens[plan.nx + 1] = zeros

    def tile_at(ref, lead, t):
        return ref[lead, :, pl.ds(pl.multiple_of(t * LANES, LANES), LANES)].astype(jnp.float32)

    def straddle(a, b):
        return pltpu.roll(jnp.where(flat_low, b, a), HALF, 1)

    def wait_layer(x):
        pltpu.make_async_copy(wbuf.at[x], wbuf.at[x], dsem.at[x]).wait()

    def spread(x):
        tiles = [tile_at(wbuf, x, jnp.maximum(off - 1, 0)) * has_left]
        tiles += [tile_at(wbuf, x, off + t) for t in range(rows)]
        tiles += [tile_at(wbuf, x, jnp.minimum(off + rows, plan.win_tiles - 1)) * has_right]
        for t in range(rows):
            here = tiles[t + 1]
            after = pltpu.roll(jnp.where(flat_first, tiles[t + 2], here), LANES - 1, 1)
            before = pltpu.roll(jnp.where(flat_last, tiles[t], here), 1, 1)
            dens[x + 1, pl.ds(t, cy, stride=rows), :] = here
            slope_z[x % 2, pl.ds(t, cy, stride=rows), :] = after - before

    def wait_occ(block):
        @pl.when(block != me_l)
        def _():
            pltpu.make_async_copy(occ.at[block], occ.at[block], osem.at[block]).wait()

    light_copy.wait()
    for c in range(3):
        for t in range(rows):
            front[c, pl.ds(t, cy, stride=rows), :] = tile_at(lbuf, c, off + t)
        for e, t in enumerate(edge_tiles):
            edge_front[e, c] = straddle(tile_at(lbuf, c, t), tile_at(lbuf, c, t + 1))

    wait_layer(0)
    spread(0)

    def do_layer(x, carry):
        block = x // plan.cx

        @pl.when(x % plan.cx == 0)
        def _():
            wait_occ(block)

        @pl.when(x + 1 < plan.nx)
        def _():
            wait_layer(x + 1)
            spread(x + 1)

        for e, t in enumerate(edge_tiles):
            cells = straddle(tile_at(wbuf, x, t), tile_at(wbuf, x, t + 1))
            held_a = occ[block, pl.ds(win + t, 1), :]
            held_b = occ[block, pl.ds(win + t + 1, 1), :]
            held = jnp.where(flat_low[:1], held_a, held_b)
            ext = jnp.log(1.0 + jnp.exp2(cubic(ext_coeffs, cells))) * held
            for c in range(3):
                prod = edge_front[e, c] * jnp.exp2(rates[c] * ext)
                seam = pltpu.roll(prod, HALF, 1)
                if e == 0:
                    edge_prod[0, c] = seam * has_left
                if e == len(edge_tiles) - 1:
                    edge_prod[1, c] = seam * has_right
                edge_front[e, c] = 0.5 * prod + 0.25 * (
                    pltpu.roll(prod, 1, 1) + pltpu.roll(prod, LANES - 1, 1)
                )

        held = occ[block, pl.ds(pl.multiple_of(me_l * rows, rows), rows), :]
        through = jnp.ones(core, jnp.float32)
        acc = [jnp.zeros(core, jnp.float32) for _ in range(3)]

        def at(layer, y):
            return dens[layer, y * rows : (y + 1) * rows, :]

        for y in range(cy):
            d = at(x + 1, y)
            gx = at(x + 2, y) - at(x, y)
            gy = at(x + 1, min(y + 1, cy - 1)) - at(x + 1, max(y - 1, 0))
            gz = slope_z[x % 2, y * rows : (y + 1) * rows, :]
            facing = (0.28 * gx + 0.126 * gy + 0.168 * gz) * lax.rsqrt(
                4.0 + gx * gx + gy * gy + gz * gz
            )
            shading = 0.65 + facing
            ext = jnp.log(1.0 + jnp.exp2(cubic(ext_coeffs, d))) * held
            passing = jnp.exp2(path_rate * ext)
            weight = jnp.where(facing_back, 1.0, through) * (1.0 - passing)
            keep = jnp.where(facing_back, passing, 1.0)
            through = through * passing
            for c in range(3):
                colour = recip(1.0 + jnp.exp2(cubic(colour_coeffs[c], d)))
                f = front[c, y * rows : (y + 1) * rows, :]
                acc[c] = keep * acc[c] + (weight * colour) * (0.2 + f * shading)
                prod = f * jnp.exp2(rates[c] * ext)
                seam_l = edge_prod[0, c, y : y + 1, :]
                seam_r = edge_prod[1, c, y : y + 1, :]
                up = jnp.where(first_row, seam_l, pltpu.roll(prod, 1, 0))
                down = jnp.where(last_row, seam_r, pltpu.roll(prod, rows - 1, 0))
                before = pltpu.roll(jnp.where(last_lane, up, prod), 1, 1)
                after = pltpu.roll(jnp.where(first_lane, down, prod), LANES - 1, 1)
                front[c, y * rows : (y + 1) * rows, :] = 0.5 * prod + 0.25 * (before + after)

        pixels = acc + [1.0 - through]
        n = plan.piece_rows
        for j in range(plan.groups):
            for c in range(4):
                image[x, j, c * n : (c + 1) * n, :] = pixels[c][j * n : (j + 1) * n, :]
        for j in range(plan.groups):
            send_piece(x, j, True)
        return carry

    def send_piece(x, j, start):
        owner_l = x // plan.cx
        owner_v = (x % plan.cx) * plan.per_layer + me_l * plan.groups + j
        mine = jnp.logical_and(owner_l == me_l, owner_v == me_v)

        @pl.when(mine)
        def _():
            if start:
                pltpu.make_async_copy(image.at[x, j], recv.at[me_v], rsem.at[me_v]).start()

        @pl.when(jnp.logical_not(mine))
        def _():
            copy = pltpu.make_async_remote_copy(
                src_ref=image.at[x, j],
                dst_ref=recv.at[me_v],
                send_sem=isend.at[x, j],
                recv_sem=rsem.at[me_v],
                device_id={"light": owner_l, "view": owner_v},
                device_id_type=MESH,
            )
            if start:
                copy.start()
            else:
                copy.wait_send()

    lax.fori_loop(0, plan.nx, do_layer, 0)

    n = plan.piece_rows
    small = (n, LANES)
    back = jnp.full(small, view_sign[0]) < 0.0

    def merge(v, carry):
        pltpu.make_async_copy(recv.at[v], recv.at[v], rsem.at[v]).wait()
        through, acc = carry[0], carry[1:]
        passing = 1.0 - recv[v, 3 * n : 4 * n, :]
        weight = jnp.where(back, 1.0, through)
        keep = jnp.where(back, passing, 1.0)
        acc = [keep * acc[c] + weight * recv[v, c * n : (c + 1) * n, :] for c in range(3)]
        return (through * passing, *acc)

    zero = jnp.zeros(small, jnp.float32)
    merged = lax.fori_loop(0, views, merge, (jnp.ones(small, jnp.float32), zero, zero, zero))
    pixels = list(merged[1:]) + [1.0 - merged[0]]
    for c in range(4):
        for r in range(n):
            out[c : c + 1, r * LANES : (r + 1) * LANES] = pixels[c][r : r + 1, :]

    def finish(x, carry):
        for j in range(plan.groups):
            send_piece(x, j, False)
        return carry

    lax.fori_loop(0, plan.nx, finish, 0)
    for k in range(1, lights):
        occ_copy(k).wait_send()
        for i in range(plan.cx):
            dens_copy(k, i).wait_send()


def body(density, occupied, view_sign, transfer, absorb, light_in):
    cells_x, cells_y, columns = density.shape
    plan = Plan(
        lax.axis_size("light"), lax.axis_size("view"), cells_x, cells_y, columns, occupied.shape[2]
    )
    lights, views = plan.lights, plan.views
    n = plan.piece_rows
    edges = 2 if lights > 2 else 1
    f32 = jnp.float32
    smem = pl.BlockSpec(memory_space=pltpu.SMEM)
    hbm = pl.BlockSpec(memory_space=pl.ANY)
    dma = pltpu.SemaphoreType.DMA
    return pl.pallas_call(
        functools.partial(kernel, plan),
        out_shape=jax.ShapeDtypeStruct((4, n * LANES), f32),
        in_specs=[hbm, smem, smem, smem, smem, hbm],
        out_specs=pl.BlockSpec(memory_space=pltpu.VMEM),
        scratch_shapes=[
            pltpu.VMEM((plan.nx, cells_y, plan.width), density.dtype),
            pltpu.VMEM((3, cells_y, plan.width), f32),
            pltpu.VMEM((lights, plan.tiles, LANES), f32),
            pltpu.VMEM((plan.nx + 2, cells_y * plan.rows, LANES), f32),
            pltpu.VMEM((2, cells_y * plan.rows, LANES), f32),
            pltpu.VMEM((3, cells_y * plan.rows, LANES), f32),
            pltpu.VMEM((edges, 3, cells_y, LANES), f32),
            pltpu.VMEM((2, 3, cells_y, LANES), f32),
            pltpu.VMEM((plan.nx, plan.groups, 4 * n, LANES), f32),
            pltpu.VMEM((views, 4 * n, LANES), f32),
            dma((plan.nx,)),
            dma((lights, cells_x)),
            dma((lights,)),
            dma((lights,)),
            dma(()),
            dma((plan.nx, plan.groups)),
            dma((views,)),
        ],
        compiler_params=pltpu.CompilerParams(
            collective_id=0, has_side_effects=True, vmem_limit_bytes=32 * 1024 * 1024
        ),
    )(density, occupied, view_sign, transfer, absorb, light_in)


def solution(mesh):
    in_specs = (
        P("light", "view", None),
        P("light", "view", None),
        P(),
        P(),
        P(),
        P(None, "view", None),
    )
    out_specs = P(None, ("light", "view"))
    return jax.shard_map(body, mesh=mesh, in_specs=in_specs, out_specs=out_specs, check_vma=False)
```

time: 65.2 us -> 20.6 us (0.32)
  the two profiles are of different devices: /device:TPU:0 before, /device:TPU:31 now
where the time goes in v1:
time: 20.6 us; the launch traced here: 20.4 us
  Pallas kernels  16.4 us (80%)
  local copies, waits for them, and re-layouts  3.23 us (16%)
  between operations  0.72 us (3%)
    pallas_call x1, Pallas kernels, body(): pl.pallas_call(functools.partial(kernel, plan), out_shape=jax.ShapeDtypeS...  16.4 us
    unnamed x11, local copies, waits for them, and re-layouts  3.23 us

profile of v1, /device:TPU:31, one launch (start us, length us, event | category | flops | bytes accessed | tf_op | source)
XLA Modules:
  0.0 20.4 jit_solution(2644777554080503252)
XLA Ops:
  0.0 0.0 copy-start.4
  0.0 0.0 copy-start.3
  0.7 0.0 copy-done.4
  0.7 0.0 copy-done.3
  0.7 0.0 copy-start
  0.7 1.0 %copy-done = f32[3,16,2048]{2,1,0:T(8,128)S(1)} copy-done((f32[3,16,2048]{2,1,0:T(8,128)S(1)}, f32[3,16,2048]{2,1,0:T(8,128)}, u32[]{:S(2)}) %copy-start) | copy-done | bytes 393240
  1.7 0.0 copy-start.1
  1.7 0.9 %copy-done.1 = bf16[4,16,2048]{2,1,0:T(8,128)(2,1)S(1)} copy-done((bf16[4,16,2048]{2,1,0:T(8,128)(2,1)S(1)}, bf16[4,16,2048]{2,1,0:T(8,128)(2,1)}, u32[]{:S(2)}) %copy-start.1) | copy-done | bytes 262168
  2.7 0.0 copy-start.2
  2.7 0.7 %copy-done.2 = f32[4,4]{1,0:T(4,128)S(1)} copy-done((f32[4,4]{1,0:T(4,128)S(1)}, f32[4,4]{1,0:T(4,128)}, u32[]{:S(2)}) %copy-start.2) | copy-done | bytes 88
  3.3 16.4 %shard_map.64 = f32[4,512]{1,0:T(4,128)S(1)} custom-call(bf16[4,16,2048]{2,1,0:T(8,128)(2,1)S(1)} %copy-done.1, s32[1,1,16]{2,1,0:T(1,128)S(1)} %copy-done.3, f32[1]{0:T(128)S(6)} %copy.8.view_sign, f32[4,4]{1,0:T(4,128)S(1)} %copy-done.2, f32[3]{0:T(128)S(1)} %copy-done.4, f32[3,16,2048]{2,1,0:T(8,128)S(1)} %copy-done), custom_call_target="tpu_custom_call" | custom-call | tf_op jit(solution)/shard_map/pallas_call | solution.py:351
  19.8 0.6 %copy.9 = f32[4,512]{1,0:T(4,128)} copy(f32[4,512]{1,0:T(4,128)S(1)} %shard_map.64) | data formatting | bytes 16384
Async XLA Ops:
  0.0 0.7 %copy-start.4 = (f32[3]{0:T(128)S(1)}, f32[3]{0:T(128)}, u32[]{:S(2)}) copy-start(f32[3]{0:T(128)} %absorb.1) | copy-start | bytes 40
  0.0 0.7 %copy-start.3 = (s32[1,1,16]{2,1,0:T(1,128)S(1)}, s32[1,1,16]{2,1,0:T(1,128)}, u32[]{:S(2)}) copy-start(s32[1,1,16]{2,1,0:T(1,128)} %occupied.1) | copy-start | bytes 196
  0.7 1.0 %copy-start = (f32[3,16,2048]{2,1,0:T(8,128)S(1)}, f32[3,16,2048]{2,1,0:T(8,128)}, u32[]{:S(2)}) copy-start(f32[3,16,2048]{2,1,0:T(8,128)} %light_in.1) | copy-start | bytes 1179652
  1.7 0.9 %copy-start.1 = (bf16[4,16,2048]{2,1,0:T(8,128)(2,1)S(1)}, bf16[4,16,2048]{2,1,0:T(8,128)(2,1)}, u32[]{:S(2)}) copy-start(bf16[4,16,2048]{2,1,0:T(8,128)(2,1)} %density.1) | copy-start | bytes 786436
  2.7 0.7 %copy-start.2 = (f32[4,4]{1,0:T(4,128)S(1)}, f32[4,4]{1,0:T(4,128)}, u32[]{:S(2)}) copy-start(f32[4,4]{1,0:T(4,128)} %transfer.1) | copy-start | bytes 196

commit v2 on v1

--- a/solution.py
+++ b/solution.py
@@ -44,12 +44,16 @@
 def kernel(
     plan,
     density,
+    occupied_hbm,
+    view_sign_hbm,
+    transfer_hbm,
+    absorb_hbm,
+    light_in,
+    out,
     occupied,
     view_sign,
     transfer,
     absorb,
-    light_in,
-    out,
     wbuf,
     lbuf,
     occ,
@@ -75,6 +79,20 @@
     off = me_l * rows - win
     slab_of_me = ((me_v * plan.piece_rows) % plan.tiles) // rows
 
+    small_copies = [
+        pltpu.make_async_copy(src, dst, lsem.at[i])
+        for i, (src, dst) in enumerate(
+            (
+                (occupied_hbm, occupied),
+                (view_sign_hbm, view_sign),
+                (transfer_hbm, transfer),
+                (absorb_hbm, absorb),
+            )
+        )
+    ]
+    for copy in small_copies:
+        copy.start()
+
     barrier = pltpu.get_barrier_semaphore()
     for k in range(1, lights):
         pl.semaphore_signal(
@@ -100,9 +118,11 @@
         pltpu.make_async_copy(
             density.at[i, :, columns_of(me_l)], wbuf.at[layer], dsem.at[layer]
         ).start()
-    light_copy = pltpu.make_async_copy(light_in.at[:, :, columns_of(me_l)], lbuf, lsem)
+    light_copy = pltpu.make_async_copy(light_in.at[:, :, columns_of(me_l)], lbuf, lsem.at[4])
     light_copy.start()
 
+    for copy in small_copies:
+        copy.wait()
     for k in range(plan.bricks):
         value = jnp.full((plan.tiles_per_brick, LANES), occupied[0, 0, k].astype(jnp.float32))
         occ[me_l, k * plan.tiles_per_brick : (k + 1) * plan.tiles_per_brick, :] = value
@@ -168,7 +188,6 @@
 
     zeros = jnp.zeros((cy * rows, LANES), jnp.float32)
     dens[0] = zeros
-    dens[plan.nx + 1] = zeros
 
     def tile_at(ref, lead, t):
         return ref[lead, :, pl.ds(pl.multiple_of(t * LANES, LANES), LANES)].astype(jnp.float32)
@@ -180,14 +199,16 @@
         pltpu.make_async_copy(wbuf.at[x], wbuf.at[x], dsem.at[x]).wait()
 
     def spread(x):
-        tiles = [tile_at(wbuf, x, jnp.maximum(off - 1, 0)) * has_left]
-        tiles += [tile_at(wbuf, x, off + t) for t in range(rows)]
-        tiles += [tile_at(wbuf, x, jnp.minimum(off + rows, plan.win_tiles - 1)) * has_right]
+        inside = jnp.where(x < plan.nx, 1.0, 0.0)
+        layer = jnp.minimum(x, plan.nx - 1)
+        tiles = [tile_at(wbuf, layer, jnp.maximum(off - 1, 0)) * has_left]
+        tiles += [tile_at(wbuf, layer, off + t) for t in range(rows)]
+        tiles += [tile_at(wbuf, layer, jnp.minimum(off + rows, plan.win_tiles - 1)) * has_right]
         for t in range(rows):
             here = tiles[t + 1]
             after = pltpu.roll(jnp.where(flat_first, tiles[t + 2], here), LANES - 1, 1)
             before = pltpu.roll(jnp.where(flat_last, tiles[t], here), 1, 1)
-            dens[x + 1, pl.ds(t, cy, stride=rows), :] = here
+            dens[x + 1, pl.ds(t, cy, stride=rows), :] = here * inside
             slope_z[x % 2, pl.ds(t, cy, stride=rows), :] = after - before
 
     def wait_occ(block):
@@ -195,30 +216,11 @@
         def _():
             pltpu.make_async_copy(occ.at[block], occ.at[block], osem.at[block]).wait()
 
-    light_copy.wait()
-    for c in range(3):
-        for t in range(rows):
-            front[c, pl.ds(t, cy, stride=rows), :] = tile_at(lbuf, c, off + t)
+    def cross(x):
+        layer = jnp.minimum(x, plan.nx - 1)
+        block = layer // plan.cx
         for e, t in enumerate(edge_tiles):
-            edge_front[e, c] = straddle(tile_at(lbuf, c, t), tile_at(lbuf, c, t + 1))
-
-    wait_layer(0)
-    spread(0)
-
-    def do_layer(x, carry):
-        block = x // plan.cx
-
-        @pl.when(x % plan.cx == 0)
-        def _():
-            wait_occ(block)
-
-        @pl.when(x + 1 < plan.nx)
-        def _():
-            wait_layer(x + 1)
-            spread(x + 1)
-
-        for e, t in enumerate(edge_tiles):
-            cells = straddle(tile_at(wbuf, x, t), tile_at(wbuf, x, t + 1))
+            cells = straddle(tile_at(wbuf, layer, t), tile_at(wbuf, layer, t + 1))
             held_a = occ[block, pl.ds(win + t, 1), :]
             held_b = occ[block, pl.ds(win + t + 1, 1), :]
             held = jnp.where(flat_low[:1], held_a, held_b)
@@ -227,19 +229,59 @@
                 prod = edge_front[e, c] * jnp.exp2(rates[c] * ext)
                 seam = pltpu.roll(prod, HALF, 1)
                 if e == 0:
-                    edge_prod[0, c] = seam * has_left
+                    edge_prod[x % 2, 0, c] = seam * has_left
                 if e == len(edge_tiles) - 1:
-                    edge_prod[1, c] = seam * has_right
+                    edge_prod[x % 2, 1, c] = seam * has_right
                 edge_front[e, c] = 0.5 * prod + 0.25 * (
                     pltpu.roll(prod, 1, 1) + pltpu.roll(prod, LANES - 1, 1)
                 )
 
+    light_copy.wait()
+    for c in range(3):
+        for t in range(rows):
+            front[c, pl.ds(t, cy, stride=rows), :] = tile_at(lbuf, c, off + t)
+        for e, t in enumerate(edge_tiles):
+            edge_front[e, c] = straddle(tile_at(lbuf, c, t), tile_at(lbuf, c, t + 1))
+
+    wait_layer(0)
+    wait_occ(0)
+    spread(0)
+    cross(0)
+
+    def do_layer(x, carry):
+        block = x // plan.cx
+
+        @pl.when(x + 1 < plan.nx)
+        def _():
+            wait_layer(x + 1)
+
+        @pl.when(jnp.logical_and(x + 1 < plan.nx, (x + 1) % plan.cx == 0))
+        def _():
+            wait_occ((x + 1) // plan.cx)
+
+        spread(x + 1)
+        cross(x + 1)
+
         held = occ[block, pl.ds(pl.multiple_of(me_l * rows, rows), rows), :]
-        through = jnp.ones(core, jnp.float32)
         acc = [jnp.zeros(core, jnp.float32) for _ in range(3)]
 
         def at(layer, y):
             return dens[layer, y * rows : (y + 1) * rows, :]
+
+        exts = [
+            jnp.log(1.0 + jnp.exp2(cubic(ext_coeffs, at(x + 1, y)))) * held for y in range(cy)
+        ]
+        passing = [jnp.exp2(path_rate * ext) for ext in exts]
+        in_front = [jnp.ones(core, jnp.float32)]
+        behind = [jnp.ones(core, jnp.float32)]
+        for y in range(cy):
+            in_front.append(in_front[-1] * passing[y])
+            behind.append(behind[-1] * passing[cy - 1 - y])
+        weights = [
+            jnp.where(facing_back, behind[cy - 1 - y], in_front[y]) * (1.0 - passing[y])
+            for y in range(cy)
+        ]
+        through = in_front[cy]
 
         for y in range(cy):
             d = at(x + 1, y)
@@ -250,18 +292,13 @@
                 4.0 + gx * gx + gy * gy + gz * gz
             )
             shading = 0.65 + facing
-            ext = jnp.log(1.0 + jnp.exp2(cubic(ext_coeffs, d))) * held
-            passing = jnp.exp2(path_rate * ext)
-            weight = jnp.where(facing_back, 1.0, through) * (1.0 - passing)
-            keep = jnp.where(facing_back, passing, 1.0)
-            through = through * passing
             for c in range(3):
                 colour = recip(1.0 + jnp.exp2(cubic(colour_coeffs[c], d)))
                 f = front[c, y * rows : (y + 1) * rows, :]
-                acc[c] = keep * acc[c] + (weight * colour) * (0.2 + f * shading)
-                prod = f * jnp.exp2(rates[c] * ext)
-                seam_l = edge_prod[0, c, y : y + 1, :]
-                seam_r = edge_prod[1, c, y : y + 1, :]
+                acc[c] = acc[c] + (weights[y] * colour) * (0.2 + f * shading)
+                prod = f * jnp.exp2(rates[c] * exts[y])
+                seam_l = edge_prod[x % 2, 0, c, y : y + 1, :]
+                seam_r = edge_prod[x % 2, 1, c, y : y + 1, :]
                 up = jnp.where(first_row, seam_l, pltpu.roll(prod, 1, 0))
                 down = jnp.where(last_row, seam_r, pltpu.roll(prod, rows - 1, 0))
                 before = pltpu.roll(jnp.where(last_lane, up, prod), 1, 1)
@@ -345,15 +382,18 @@
     n = plan.piece_rows
     edges = 2 if lights > 2 else 1
     f32 = jnp.float32
-    smem = pl.BlockSpec(memory_space=pltpu.SMEM)
     hbm = pl.BlockSpec(memory_space=pl.ANY)
     dma = pltpu.SemaphoreType.DMA
     return pl.pallas_call(
         functools.partial(kernel, plan),
         out_shape=jax.ShapeDtypeStruct((4, n * LANES), f32),
-        in_specs=[hbm, smem, smem, smem, smem, hbm],
+        in_specs=[hbm] * 6,
         out_specs=pl.BlockSpec(memory_space=pltpu.VMEM),
         scratch_shapes=[
+            pltpu.SMEM(occupied.shape, occupied.dtype),
+            pltpu.SMEM(view_sign.shape, f32),
+            pltpu.SMEM(transfer.shape, f32),
+            pltpu.SMEM(absorb.shape, f32),
             pltpu.VMEM((plan.nx, cells_y, plan.width), density.dtype),
             pltpu.VMEM((3, cells_y, plan.width), f32),
             pltpu.VMEM((lights, plan.tiles, LANES), f32),
@@ -361,19 +401,19 @@
             pltpu.VMEM((2, cells_y * plan.rows, LANES), f32),
             pltpu.VMEM((3, cells_y * plan.rows, LANES), f32),
             pltpu.VMEM((edges, 3, cells_y, LANES), f32),
-            pltpu.VMEM((2, 3, cells_y, LANES), f32),
+            pltpu.VMEM((2, 2, 3, cells_y, LANES), f32),
             pltpu.VMEM((plan.nx, plan.groups, 4 * n, LANES), f32),
             pltpu.VMEM((views, 4 * n, LANES), f32),
             dma((plan.nx,)),
             dma((lights, cells_x)),
             dma((lights,)),
             dma((lights,)),
-            dma(()),
+            dma((5,)),
             dma((plan.nx, plan.groups)),
             dma((views,)),
         ],
         compiler_params=pltpu.CompilerParams(
-            collective_id=0, has_side_effects=True, vmem_limit_bytes=32 * 1024 * 1024
+            collective_id=0, has_side_effects=True
         ),
     )(density, occupied, view_sign, transfer, absorb, light_in)
 

time: 20.6 us -> 17.8 us (0.86)
  local copies, waits for them, and re-layouts: 3.23 us -> 1.3 us
  Pallas kernels: 16.4 us -> 15.6 us
    unnamed x11 -> x1, local copies, waits for them, and re-layouts: 3.23 us -> 1.3 us
    pallas_call x1, Pallas kernels: 16.4 us -> 15.6 us  [body(): pl.pallas_call(functools.partial(kernel, plan), out_shape=jax.ShapeDtypeS...]
where the time goes in v2:
time: 17.8 us; the launch traced here: 17.6 us
  Pallas kernels  15.6 us (88%)
  local copies, waits for them, and re-layouts  1.3 us (7%)
  between operations  0.66 us (4%)
    pallas_call x1, Pallas kernels, body(): pl.pallas_call(functools.partial(kernel, plan), out_shape=jax.ShapeDtypeS...  15.6 us
    unnamed x1, local copies, waits for them, and re-layouts  1.3 us

profile of v2, /device:TPU:31, one launch (start us, length us, event | category | flops | bytes accessed | tf_op | source)
XLA Modules:
  0.0 17.6 jit_solution(8073258427060589356)
XLA Ops:
  0.7 15.6 %shard_map.64 = f32[4,512]{1,0:T(4,128)} custom-call(bf16[4,16,2048]{2,1,0:T(8,128)(2,1)} %density.1, s32[1,1,16]{2,1,0:T(1,128)} %occupied_hbm.1, f32[1]{0:T(128)S(6)} %copy.8.view_sign_hbm, f32[4,4]{1,0:T(4,128)} %transfer_hbm.1, f32[3]{0:T(128)} %absorb_hbm.1, f32[3,16,2048]{2,1,0:T(8,128)} %light_in.1), custom_call_target="tpu_custom_call" | custom-call | tf_op jit(solution)/shard_map/pallas_call | solution.py:387
  16.3 1.3 %copy.9 = f32[4,512]{1,0:T(4,128)} copy(f32[4,512]{1,0:T(4,128)} %shard_map.64) | data formatting | bytes 16384

commit v3 on v2

--- a/solution.py
+++ b/solution.py
@@ -9,7 +9,6 @@
 
 LANES = 128
 HALF = LANES // 2
-LOG2E = 1.4426950408889634
 MESH = pl.DeviceIdType.MESH
 
 
@@ -34,11 +33,6 @@
 
 def cubic(coeffs, x):
     return coeffs[0] + x * (coeffs[1] + x * (coeffs[2] + x * coeffs[3]))
-
-
-def recip(x):
-    r = pltpu.reciprocal(x, approx=True)
-    return r * (2.0 - x * r)
 
 
 def kernel(
@@ -59,6 +53,9 @@
     occ,
     dens,
     slope_z,
+    transmit,
+    lit,
+    base,
     front,
     edge_front,
     edge_prod,
@@ -172,19 +169,18 @@
     flat_lane = lax.broadcasted_iota(jnp.int32, flat, 1)
     flat_first, flat_last = flat_lane == 0, flat_lane == LANES - 1
     flat_low = flat_lane < HALF
-    sign = jnp.full(core, view_sign[0])
+    sign = jnp.full(core, view_sign[0, 0])
     facing_back = sign < 0.0
-    path_rate = (-2.0 * LOG2E / plan.ny) / jnp.abs(sign)
-    rates = [absorb[c] * (-LOG2E / plan.nx) for c in range(3)]
-    ext_coeffs = [transfer[0, k] * LOG2E for k in range(4)]
-    colour_coeffs = [[transfer[c, k] * (-LOG2E) for k in range(4)] for c in (1, 2, 3)]
+    path_rate = (-2.0 / plan.ny) / jnp.abs(sign)
+    rates = [absorb[c] * (-1.0 / plan.nx) for c in range(3)]
+    ext_coeffs = [transfer[0, k] for k in range(4)]
+    colour_coeffs = [[transfer[c, k] * 0.5 for k in range(4)] for c in (1, 2, 3)]
     has_left = jnp.where(me_l > 0, 1.0, 0.0)
     has_right = jnp.where(me_l < lights - 1, 1.0, 0.0)
-    edge_tiles = [jnp.maximum(off - 1, 0)]
+    edge_tiles = [jnp.where(me_l == 0, rows - 1, 0)]
     if lights > 2:
         edge_tiles = [jnp.maximum(off - 1, 0), jnp.minimum(off + rows - 1, plan.win_tiles - 2)]
-    else:
-        edge_tiles = [jnp.where(me_l == 0, rows - 1, 0)]
+    seam_mask = jnp.where(flat_low, has_right, has_left)
 
     zeros = jnp.zeros((cy * rows, LANES), jnp.float32)
     dens[0] = zeros
@@ -209,7 +205,7 @@
             after = pltpu.roll(jnp.where(flat_first, tiles[t + 2], here), LANES - 1, 1)
             before = pltpu.roll(jnp.where(flat_last, tiles[t], here), 1, 1)
             dens[x + 1, pl.ds(t, cy, stride=rows), :] = here * inside
-            slope_z[x % 2, pl.ds(t, cy, stride=rows), :] = after - before
+            slope_z[layer, pl.ds(t, cy, stride=rows), :] = after - before
 
     def wait_occ(block):
         @pl.when(block != me_l)
@@ -219,100 +215,85 @@
     def cross(x):
         layer = jnp.minimum(x, plan.nx - 1)
         block = layer // plan.cx
+        seams = [[] for _ in range(3)]
         for e, t in enumerate(edge_tiles):
             cells = straddle(tile_at(wbuf, layer, t), tile_at(wbuf, layer, t + 1))
             held_a = occ[block, pl.ds(win + t, 1), :]
             held_b = occ[block, pl.ds(win + t + 1, 1), :]
             held = jnp.where(flat_low[:1], held_a, held_b)
-            ext = jnp.log(1.0 + jnp.exp2(cubic(ext_coeffs, cells))) * held
+            ext = jnp.log(1.0 + jnp.exp(cubic(ext_coeffs, cells))) * held
             for c in range(3):
-                prod = edge_front[e, c] * jnp.exp2(rates[c] * ext)
-                seam = pltpu.roll(prod, HALF, 1)
-                if e == 0:
-                    edge_prod[x % 2, 0, c] = seam * has_left
-                if e == len(edge_tiles) - 1:
-                    edge_prod[x % 2, 1, c] = seam * has_right
+                prod = edge_front[e, c] * jnp.exp(rates[c] * ext)
+                seams[c].append(pltpu.roll(prod, HALF, 1))
                 edge_front[e, c] = 0.5 * prod + 0.25 * (
                     pltpu.roll(prod, 1, 1) + pltpu.roll(prod, LANES - 1, 1)
                 )
-
-    light_copy.wait()
-    for c in range(3):
-        for t in range(rows):
-            front[c, pl.ds(t, cy, stride=rows), :] = tile_at(lbuf, c, off + t)
-        for e, t in enumerate(edge_tiles):
-            edge_front[e, c] = straddle(tile_at(lbuf, c, t), tile_at(lbuf, c, t + 1))
-
-    wait_layer(0)
-    wait_occ(0)
-    spread(0)
-    cross(0)
-
-    def do_layer(x, carry):
-        block = x // plan.cx
-
-        @pl.when(x + 1 < plan.nx)
-        def _():
-            wait_layer(x + 1)
-
-        @pl.when(jnp.logical_and(x + 1 < plan.nx, (x + 1) % plan.cx == 0))
-        def _():
-            wait_occ((x + 1) // plan.cx)
-
-        spread(x + 1)
-        cross(x + 1)
-
-        held = occ[block, pl.ds(pl.multiple_of(me_l * rows, rows), rows), :]
-        acc = [jnp.zeros(core, jnp.float32) for _ in range(3)]
+        for c in range(3):
+            seam = seams[c][0]
+            if len(edge_tiles) > 1:
+                seam = jnp.where(flat_low, seams[c][1], seam)
+            edge_prod[x % 2, c] = seam * seam_mask
+
+    def cells_of(y):
+        return slice(y * rows, (y + 1) * rows)
+
+    def prepare(x):
+        held = occ[x // plan.cx, pl.ds(pl.multiple_of(me_l * rows, rows), rows), :]
 
         def at(layer, y):
-            return dens[layer, y * rows : (y + 1) * rows, :]
-
-        exts = [
-            jnp.log(1.0 + jnp.exp2(cubic(ext_coeffs, at(x + 1, y)))) * held for y in range(cy)
-        ]
-        passing = [jnp.exp2(path_rate * ext) for ext in exts]
-        in_front = [jnp.ones(core, jnp.float32)]
-        behind = [jnp.ones(core, jnp.float32)]
+            return dens[layer, cells_of(y), :]
+
+        passing = []
         for y in range(cy):
-            in_front.append(in_front[-1] * passing[y])
-            behind.append(behind[-1] * passing[cy - 1 - y])
-        weights = [
-            jnp.where(facing_back, behind[cy - 1 - y], in_front[y]) * (1.0 - passing[y])
-            for y in range(cy)
-        ]
-        through = in_front[cy]
-
+            ext = jnp.log(1.0 + jnp.exp(cubic(ext_coeffs, at(x + 1, y)))) * held
+            passing.append(jnp.exp(path_rate * ext))
+            for c in range(3):
+                transmit[x, c, cells_of(y), :] = jnp.exp(rates[c] * ext)
+        behind = [jnp.full(core, 0.5)]
+        for y in reversed(range(1, cy)):
+            behind.append(behind[-1] * passing[y])
+        in_front = jnp.full(core, 0.5)
+        ambient = [jnp.zeros(core, jnp.float32) for _ in range(3)]
         for y in range(cy):
+            seen = jnp.where(facing_back, behind[cy - 1 - y], in_front) * (1.0 - passing[y])
+            in_front = in_front * passing[y]
             d = at(x + 1, y)
             gx = at(x + 2, y) - at(x, y)
             gy = at(x + 1, min(y + 1, cy - 1)) - at(x + 1, max(y - 1, 0))
-            gz = slope_z[x % 2, y * rows : (y + 1) * rows, :]
+            gz = slope_z[x, cells_of(y), :]
             facing = (0.28 * gx + 0.126 * gy + 0.168 * gz) * lax.rsqrt(
                 4.0 + gx * gx + gy * gy + gz * gz
             )
             shading = 0.65 + facing
             for c in range(3):
-                colour = recip(1.0 + jnp.exp2(cubic(colour_coeffs[c], d)))
-                f = front[c, y * rows : (y + 1) * rows, :]
-                acc[c] = acc[c] + (weights[y] * colour) * (0.2 + f * shading)
-                prod = f * jnp.exp2(rates[c] * exts[y])
-                seam_l = edge_prod[x % 2, 0, c, y : y + 1, :]
-                seam_r = edge_prod[x % 2, 1, c, y : y + 1, :]
-                up = jnp.where(first_row, seam_l, pltpu.roll(prod, 1, 0))
-                down = jnp.where(last_row, seam_r, pltpu.roll(prod, rows - 1, 0))
+                coloured = seen * (1.0 + jnp.tanh(cubic(colour_coeffs[c], d)))
+                ambient[c] = ambient[c] + coloured
+                lit[x, c, cells_of(y), :] = coloured * shading
+        for c in range(3):
+            base[x, c] = 0.2 * ambient[c]
+        base[x, 3] = 1.0 - 2.0 * in_front
+
+    def shine(x):
+        pixels = [base[x, c] for c in range(4)]
+        for y in range(cy):
+            for c in range(3):
+                f = front[c, cells_of(y), :]
+                pixels[c] = pixels[c] + f * lit[x, c, cells_of(y), :]
+                prod = f * transmit[x, c, cells_of(y), :]
+                seam = edge_prod[x % 2, c, y : y + 1, :]
+                up = jnp.where(first_row, seam, pltpu.roll(prod, 1, 0))
+                down = jnp.where(last_row, seam, pltpu.roll(prod, rows - 1, 0))
                 before = pltpu.roll(jnp.where(last_lane, up, prod), 1, 1)
                 after = pltpu.roll(jnp.where(first_lane, down, prod), LANES - 1, 1)
-                front[c, y * rows : (y + 1) * rows, :] = 0.5 * prod + 0.25 * (before + after)
-
-        pixels = acc + [1.0 - through]
+                front[c, cells_of(y), :] = 0.5 * prod + 0.25 * (before + after)
         n = plan.piece_rows
         for j in range(plan.groups):
             for c in range(4):
                 image[x, j, c * n : (c + 1) * n, :] = pixels[c][j * n : (j + 1) * n, :]
+
+    def send_layer(x):
         for j in range(plan.groups):
             send_piece(x, j, True)
-        return carry
 
     def send_piece(x, j, start):
         owner_l = x // plan.cx
@@ -339,11 +320,76 @@
             else:
                 copy.wait_send()
 
-    lax.fori_loop(0, plan.nx, do_layer, 0)
+    start = jnp.where(me_l > 0, me_l * plan.cx + 1, 0)
+    lead = jnp.where(me_l > 0, plan.nx - start, 0)
+
+    light_copy.wait()
+    for c in range(3):
+        for t in range(rows):
+            front[c, pl.ds(t, cy, stride=rows), :] = tile_at(lbuf, c, off + t)
+        for e, t in enumerate(edge_tiles):
+            edge_front[e, c] = straddle(tile_at(lbuf, c, t), tile_at(lbuf, c, t + 1))
+
+    @pl.when(me_l > 0)
+    def _():
+        wait_layer(start - 1)
+        spread(start - 1)
+
+    wait_layer(start)
+    spread(start)
+
+    @pl.when(me_l == 0)
+    def _():
+        cross(0)
+
+    def arrive(x):
+        new = jnp.logical_and(x < plan.nx, jnp.logical_and(x != start, x != start - 1))
+
+        @pl.when(new)
+        def _():
+            wait_layer(x)
+
+        @pl.when(jnp.logical_and(new, x % plan.cx == 0))
+        def _():
+            wait_occ(x // plan.cx)
+
+    def early(step, carry):
+        x = start + step
+        arrive(x + 1)
+        spread(x + 1)
+        prepare(x)
+        return carry
+
+    def both(step, carry):
+        x = (start + step) % plan.nx
+
+        @pl.when(jnp.logical_and(x == 0, step > 0))
+        def _():
+            arrive(0)
+            spread(0)
+            cross(0)
+
+        arrive(x + 1)
+        spread(x + 1)
+        cross(x + 1)
+        prepare(x)
+        shine(x)
+        send_layer(x)
+        return carry
+
+    def late(x, carry):
+        cross(x + 1)
+        shine(x)
+        send_layer(x)
+        return carry
+
+    lax.fori_loop(0, lead, early, 0)
+    lax.fori_loop(lead, plan.nx, both, 0)
+    lax.fori_loop(plan.nx - lead, plan.nx, late, 0)
 
     n = plan.piece_rows
     small = (n, LANES)
-    back = jnp.full(small, view_sign[0]) < 0.0
+    back = jnp.full(small, view_sign[0, 0]) < 0.0
 
     def merge(v, carry):
         pltpu.make_async_copy(recv.at[v], recv.at[v], rsem.at[v]).wait()
@@ -391,17 +437,20 @@
         out_specs=pl.BlockSpec(memory_space=pltpu.VMEM),
         scratch_shapes=[
             pltpu.SMEM(occupied.shape, occupied.dtype),
-            pltpu.SMEM(view_sign.shape, f32),
+            pltpu.SMEM((1, 1), f32),
             pltpu.SMEM(transfer.shape, f32),
             pltpu.SMEM(absorb.shape, f32),
             pltpu.VMEM((plan.nx, cells_y, plan.width), density.dtype),
             pltpu.VMEM((3, cells_y, plan.width), f32),
             pltpu.VMEM((lights, plan.tiles, LANES), f32),
             pltpu.VMEM((plan.nx + 2, cells_y * plan.rows, LANES), f32),
-            pltpu.VMEM((2, cells_y * plan.rows, LANES), f32),
+            pltpu.VMEM((plan.nx, cells_y * plan.rows, LANES), f32),
+            pltpu.VMEM((plan.nx, 3, cells_y * plan.rows, LANES), f32),
+            pltpu.VMEM((plan.nx, 3, cells_y * plan.rows, LANES), f32),
+            pltpu.VMEM((plan.nx, 4, plan.rows, LANES), f32),
             pltpu.VMEM((3, cells_y * plan.rows, LANES), f32),
             pltpu.VMEM((edges, 3, cells_y, LANES), f32),
-            pltpu.VMEM((2, 2, 3, cells_y, LANES), f32),
+            pltpu.VMEM((2, 3, cells_y, LANES), f32),
             pltpu.VMEM((plan.nx, plan.groups, 4 * n, LANES), f32),
             pltpu.VMEM((views, 4 * n, LANES), f32),
             dma((plan.nx,)),
@@ -415,7 +464,7 @@
         compiler_params=pltpu.CompilerParams(
             collective_id=0, has_side_effects=True
         ),
-    )(density, occupied, view_sign, transfer, absorb, light_in)
+    )(density, occupied, view_sign.reshape(1, 1), transfer, absorb, light_in)
 
 
 def solution(mesh):

time: 17.8 us -> 17.9 us (level)
  no operation moved by 1% of the time
where the time goes in v3:
time: 17.9 us; the launch traced here: 17.7 us
  Pallas kernels  15.7 us (88%)
  local copies, waits for them, and re-layouts  1.3 us (7%)
  between operations  0.66 us (4%)
    pallas_call x1, Pallas kernels, body(): pl.pallas_call(functools.partial(kernel, plan), out_shape=jax.ShapeDtypeS...  15.7 us
    unnamed x1, local copies, waits for them, and re-layouts  1.3 us

profile of v3, /device:TPU:31, one launch (start us, length us, event | category | flops | bytes accessed | tf_op | source)
XLA Modules:
  0.0 17.7 jit_solution(3511263657345720628)
XLA Ops:
  0.7 15.7 %shard_map.64 = f32[4,512]{1,0:T(4,128)} custom-call(bf16[4,16,2048]{2,1,0:T(8,128)(2,1)} %density.1, s32[1,1,16]{2,1,0:T(1,128)} %occupied_hbm.1, f32[1,1]{1,0:T(1,128)} %bitcast.1.view_sign_hbm, f32[4,4]{1,0:T(4,128)} %transfer_hbm.1, f32[3]{0:T(128)} %absorb_hbm.1, f32[3,16,2048]{2,1,0:T(8,128)} %light_in.1), custom_call_target="tpu_custom_call" | custom-call | tf_op jit(solution)/shard_map/pallas_call | solution.py:433
  16.4 1.3 %copy.9 = f32[4,512]{1,0:T(4,128)} copy(f32[4,512]{1,0:T(4,128)} %shard_map.64) | data formatting | bytes 16384

commit v4 on v3

--- a/solution.py
+++ b/solution.py
@@ -8,7 +8,6 @@
 from jax.sharding import PartitionSpec as P
 
 LANES = 128
-HALF = LANES // 2
 MESH = pl.DeviceIdType.MESH
 
 
@@ -51,14 +50,12 @@
     wbuf,
     lbuf,
     occ,
-    dens,
-    slope_z,
+    exts,
     transmit,
     lit,
     base,
+    column,
     front,
-    edge_front,
-    edge_prod,
     image,
     recv,
     dsem,
@@ -113,7 +110,7 @@
     for i in range(plan.cx):
         layer = me_l * plan.cx + i
         pltpu.make_async_copy(
-            density.at[i, :, columns_of(me_l)], wbuf.at[layer], dsem.at[layer]
+            density.at[i, :, columns_of(me_l)], wbuf.at[layer + 1], dsem.at[layer]
         ).start()
     light_copy = pltpu.make_async_copy(light_in.at[:, :, columns_of(me_l)], lbuf, lsem.at[4])
     light_copy.start()
@@ -147,7 +144,7 @@
         layer = me_l * plan.cx + i
         return pltpu.make_async_remote_copy(
             src_ref=density.at[i, :, columns_of(other)],
-            dst_ref=wbuf.at[layer],
+            dst_ref=wbuf.at[layer + 1],
             send_sem=dsend.at[k, i],
             recv_sem=dsem.at[layer],
             device_id={"light": other, "view": me_v},
@@ -160,132 +157,111 @@
         for k in range(1, lights):
             dens_copy(k, i).start()
 
-    core = (rows, LANES)
-    lane = lax.broadcasted_iota(jnp.int32, core, 1)
-    sub = lax.broadcasted_iota(jnp.int32, core, 0)
+    tile_shape = (cy, LANES)
+    lane = lax.broadcasted_iota(jnp.int32, tile_shape, 1)
     first_lane, last_lane = lane == 0, lane == LANES - 1
-    first_row, last_row = sub == 0, sub == rows - 1
-    flat = (cy, LANES)
-    flat_lane = lax.broadcasted_iota(jnp.int32, flat, 1)
-    flat_first, flat_last = flat_lane == 0, flat_lane == LANES - 1
-    flat_low = flat_lane < HALF
-    sign = jnp.full(core, view_sign[0, 0])
-    facing_back = sign < 0.0
+    sign = jnp.full(tile_shape, view_sign[0, 0])
     path_rate = (-2.0 / plan.ny) / jnp.abs(sign)
     rates = [absorb[c] * (-1.0 / plan.nx) for c in range(3)]
     ext_coeffs = [transfer[0, k] for k in range(4)]
     colour_coeffs = [[transfer[c, k] * 0.5 for k in range(4)] for c in (1, 2, 3)]
     has_left = jnp.where(me_l > 0, 1.0, 0.0)
     has_right = jnp.where(me_l < lights - 1, 1.0, 0.0)
-    edge_tiles = [jnp.where(me_l == 0, rows - 1, 0)]
-    if lights > 2:
-        edge_tiles = [jnp.maximum(off - 1, 0), jnp.minimum(off + rows - 1, plan.win_tiles - 2)]
-    seam_mask = jnp.where(flat_low, has_right, has_left)
-
-    zeros = jnp.zeros((cy * rows, LANES), jnp.float32)
-    dens[0] = zeros
+
+    to = lax.broadcasted_iota(jnp.int32, (cy, cy), 0)
+    of = lax.broadcasted_iota(jnp.int32, (cy, cy), 1)
+    after_y = (of == jnp.minimum(to + 1, cy - 1)).astype(jnp.float32)
+    before_y = (of == jnp.maximum(to - 1, 0)).astype(jnp.float32)
+    slope_y = (after_y - before_y).astype(jnp.bfloat16)
+    to = lax.broadcasted_iota(jnp.int32, (cy + 8, 2 * cy), 0)
+    of = lax.broadcasted_iota(jnp.int32, (cy + 8, 2 * cy), 1) % cy
+    one, none = jnp.ones(to.shape, jnp.float32), jnp.zeros(to.shape, jnp.float32)
+    near_first = jnp.where(of < to, one, none)
+    near_last = jnp.where(of > to, one, none)
+    sign_wide = jnp.full(to.shape, view_sign[0, 0])
+    in_front = jnp.where(sign_wide < 0.0, near_last, near_first)
+    in_front = jnp.where(to >= cy, one, in_front).astype(jnp.bfloat16)
+
+    blank = jnp.zeros((cy, plan.width), wbuf.dtype)
+    wbuf[0] = blank
+    wbuf[plan.nx + 1] = blank
 
     def tile_at(ref, lead, t):
         return ref[lead, :, pl.ds(pl.multiple_of(t * LANES, LANES), LANES)].astype(jnp.float32)
 
-    def straddle(a, b):
-        return pltpu.roll(jnp.where(flat_low, b, a), HALF, 1)
+    def next_to(left, here, right):
+        before = pltpu.roll(jnp.where(last_lane, left, here), 1, 1)
+        after = pltpu.roll(jnp.where(first_lane, right, here), LANES - 1, 1)
+        return before, after
 
     def wait_layer(x):
-        pltpu.make_async_copy(wbuf.at[x], wbuf.at[x], dsem.at[x]).wait()
-
-    def spread(x):
-        inside = jnp.where(x < plan.nx, 1.0, 0.0)
-        layer = jnp.minimum(x, plan.nx - 1)
-        tiles = [tile_at(wbuf, layer, jnp.maximum(off - 1, 0)) * has_left]
-        tiles += [tile_at(wbuf, layer, off + t) for t in range(rows)]
-        tiles += [tile_at(wbuf, layer, jnp.minimum(off + rows, plan.win_tiles - 1)) * has_right]
-        for t in range(rows):
-            here = tiles[t + 1]
-            after = pltpu.roll(jnp.where(flat_first, tiles[t + 2], here), LANES - 1, 1)
-            before = pltpu.roll(jnp.where(flat_last, tiles[t], here), 1, 1)
-            dens[x + 1, pl.ds(t, cy, stride=rows), :] = here * inside
-            slope_z[layer, pl.ds(t, cy, stride=rows), :] = after - before
+        pltpu.make_async_copy(wbuf.at[x + 1], wbuf.at[x + 1], dsem.at[x]).wait()
 
     def wait_occ(block):
         @pl.when(block != me_l)
         def _():
             pltpu.make_async_copy(occ.at[block], occ.at[block], osem.at[block]).wait()
 
-    def cross(x):
-        layer = jnp.minimum(x, plan.nx - 1)
-        block = layer // plan.cx
-        seams = [[] for _ in range(3)]
-        for e, t in enumerate(edge_tiles):
-            cells = straddle(tile_at(wbuf, layer, t), tile_at(wbuf, layer, t + 1))
-            held_a = occ[block, pl.ds(win + t, 1), :]
-            held_b = occ[block, pl.ds(win + t + 1, 1), :]
-            held = jnp.where(flat_low[:1], held_a, held_b)
+    def prepare(x):
+        block = x // plan.cx
+        for t in range(plan.win_tiles):
+            held = occ[block, pl.ds(win + t, 1), :]
+            cells = tile_at(wbuf, x + 1, t)
             ext = jnp.log(1.0 + jnp.exp(cubic(ext_coeffs, cells))) * held
+            exts[t] = ext
             for c in range(3):
-                prod = edge_front[e, c] * jnp.exp(rates[c] * ext)
-                seams[c].append(pltpu.roll(prod, HALF, 1))
-                edge_front[e, c] = 0.5 * prod + 0.25 * (
-                    pltpu.roll(prod, 1, 1) + pltpu.roll(prod, LANES - 1, 1)
-                )
-        for c in range(3):
-            seam = seams[c][0]
-            if len(edge_tiles) > 1:
-                seam = jnp.where(flat_low, seams[c][1], seam)
-            edge_prod[x % 2, c] = seam * seam_mask
-
-    def cells_of(y):
-        return slice(y * rows, (y + 1) * rows)
-
-    def prepare(x):
-        held = occ[x // plan.cx, pl.ds(pl.multiple_of(me_l * rows, rows), rows), :]
-
-        def at(layer, y):
-            return dens[layer, cells_of(y), :]
-
-        passing = []
-        for y in range(cy):
-            ext = jnp.log(1.0 + jnp.exp(cubic(ext_coeffs, at(x + 1, y)))) * held
-            passing.append(jnp.exp(path_rate * ext))
-            for c in range(3):
-                transmit[x, c, cells_of(y), :] = jnp.exp(rates[c] * ext)
-        behind = [jnp.full(core, 0.5)]
-        for y in reversed(range(1, cy)):
-            behind.append(behind[-1] * passing[y])
-        in_front = jnp.full(core, 0.5)
-        ambient = [jnp.zeros(core, jnp.float32) for _ in range(3)]
-        for y in range(cy):
-            seen = jnp.where(facing_back, behind[cy - 1 - y], in_front) * (1.0 - passing[y])
-            in_front = in_front * passing[y]
-            d = at(x + 1, y)
-            gx = at(x + 2, y) - at(x, y)
-            gy = at(x + 1, min(y + 1, cy - 1)) - at(x + 1, max(y - 1, 0))
-            gz = slope_z[x, cells_of(y), :]
-            facing = (0.28 * gx + 0.126 * gy + 0.168 * gz) * lax.rsqrt(
+                transmit[x, c, t] = jnp.exp(rates[c] * ext)
+        depths = [path_rate * exts[off + t] for t in range(rows)]
+        high = [depth.astype(jnp.bfloat16) for depth in depths]
+        low = [
+            (depth - h.astype(jnp.float32)).astype(jnp.bfloat16) for depth, h in zip(depths, high)
+        ]
+        stacked = jnp.concatenate(
+            [jnp.concatenate(high, axis=1), jnp.concatenate(low, axis=1)], axis=0
+        )
+        sums = jnp.dot(in_front, stacked, preferred_element_type=jnp.float32)
+        own = wbuf[x + 1, :, pl.ds(pl.multiple_of(off * LANES, LANES), rows * LANES)]
+        grad_y = jnp.dot(slope_y, own, preferred_element_type=jnp.float32)
+        tiles = [tile_at(wbuf, x + 1, jnp.maximum(off - 1, 0)) * has_left]
+        tiles += [tile_at(wbuf, x + 1, off + t) for t in range(rows)]
+        tiles += [tile_at(wbuf, x + 1, jnp.minimum(off + rows, plan.win_tiles - 1)) * has_right]
+        for t in range(rows):
+            part = slice(t * LANES, (t + 1) * LANES)
+            seen = jnp.exp(sums[:cy, part]) * (1.0 - jnp.exp(depths[t]))
+            d = tiles[t + 1]
+            before, after = next_to(tiles[t], d, tiles[t + 2])
+            gx = tile_at(wbuf, x + 2, off + t) - tile_at(wbuf, x, off + t)
+            gy = grad_y[:, part]
+            gz = after - before
+            facing = (0.14 * gx + 0.063 * gy + 0.084 * gz) * lax.rsqrt(
                 4.0 + gx * gx + gy * gy + gz * gz
             )
-            shading = 0.65 + facing
+            shading = 0.325 + facing
             for c in range(3):
                 coloured = seen * (1.0 + jnp.tanh(cubic(colour_coeffs[c], d)))
-                ambient[c] = ambient[c] + coloured
-                lit[x, c, cells_of(y), :] = coloured * shading
+                lit[x, c, t] = coloured * shading
+                base[x, c, t * 8 : (t + 1) * 8, :] = 0.1 * sum(
+                    coloured[k : k + 8] for k in range(0, cy, 8)
+                )
+            base[x, 3, t * 8 : (t + 1) * 8, :] = 1.0 - jnp.exp(sums[cy:, part])
+
+    def shine(x):
+        pixels = []
         for c in range(3):
-            base[x, c] = 0.2 * ambient[c]
-        base[x, 3] = 1.0 - 2.0 * in_front
-
-    def shine(x):
-        pixels = [base[x, c] for c in range(4)]
-        for y in range(cy):
-            for c in range(3):
-                f = front[c, cells_of(y), :]
-                pixels[c] = pixels[c] + f * lit[x, c, cells_of(y), :]
-                prod = f * transmit[x, c, cells_of(y), :]
-                seam = edge_prod[x % 2, c, y : y + 1, :]
-                up = jnp.where(first_row, seam, pltpu.roll(prod, 1, 0))
-                down = jnp.where(last_row, seam, pltpu.roll(prod, rows - 1, 0))
-                before = pltpu.roll(jnp.where(last_lane, up, prod), 1, 1)
-                after = pltpu.roll(jnp.where(first_lane, down, prod), LANES - 1, 1)
-                front[c, cells_of(y), :] = 0.5 * prod + 0.25 * (before + after)
+            for t in range(rows):
+                share = front[c, off + t] * lit[x, c, t]
+                column[c, t * 8 : (t + 1) * 8, :] = base[x, c, t * 8 : (t + 1) * 8, :] + sum(
+                    share[k : k + 8] for k in range(0, cy, 8)
+                )
+            prods = [front[c, t] * transmit[x, c, t] for t in range(plan.win_tiles)]
+            outside = jnp.zeros(tile_shape, jnp.float32)
+            prods = [outside] + prods + [outside]
+            for t in range(plan.win_tiles):
+                before, after = next_to(prods[t], prods[t + 1], prods[t + 2])
+                front[c, t] = 0.5 * prods[t + 1] + 0.25 * (before + after)
+        for c in range(3):
+            pixels.append(sum(column[c, pl.ds(r, rows, stride=8), :] for r in range(8)))
+        pixels.append(base[x, 3, pl.ds(0, rows, stride=8), :])
         n = plan.piece_rows
         for j in range(plan.groups):
             for c in range(4):
@@ -325,22 +301,14 @@
 
     light_copy.wait()
     for c in range(3):
-        for t in range(rows):
-            front[c, pl.ds(t, cy, stride=rows), :] = tile_at(lbuf, c, off + t)
-        for e, t in enumerate(edge_tiles):
-            edge_front[e, c] = straddle(tile_at(lbuf, c, t), tile_at(lbuf, c, t + 1))
+        for t in range(plan.win_tiles):
+            front[c, t] = lbuf[c, :, t * LANES : (t + 1) * LANES]
 
     @pl.when(me_l > 0)
     def _():
         wait_layer(start - 1)
-        spread(start - 1)
 
     wait_layer(start)
-    spread(start)
-
-    @pl.when(me_l == 0)
-    def _():
-        cross(0)
 
     def arrive(x):
         new = jnp.logical_and(x < plan.nx, jnp.logical_and(x != start, x != start - 1))
@@ -356,7 +324,6 @@
     def early(step, carry):
         x = start + step
         arrive(x + 1)
-        spread(x + 1)
         prepare(x)
         return carry
 
@@ -366,19 +333,14 @@
         @pl.when(jnp.logical_and(x == 0, step > 0))
         def _():
             arrive(0)
-            spread(0)
-            cross(0)
 
         arrive(x + 1)
-        spread(x + 1)
-        cross(x + 1)
         prepare(x)
         shine(x)
         send_layer(x)
         return carry
 
     def late(x, carry):
-        cross(x + 1)
         shine(x)
         send_layer(x)
         return carry
@@ -426,7 +388,6 @@
     )
     lights, views = plan.lights, plan.views
     n = plan.piece_rows
-    edges = 2 if lights > 2 else 1
     f32 = jnp.float32
     hbm = pl.BlockSpec(memory_space=pl.ANY)
     dma = pltpu.SemaphoreType.DMA
@@ -440,17 +401,15 @@
             pltpu.SMEM((1, 1), f32),
             pltpu.SMEM(transfer.shape, f32),
             pltpu.SMEM(absorb.shape, f32),
-            pltpu.VMEM((plan.nx, cells_y, plan.width), density.dtype),
+            pltpu.VMEM((plan.nx + 2, cells_y, plan.width), density.dtype),
             pltpu.VMEM((3, cells_y, plan.width), f32),
             pltpu.VMEM((lights, plan.tiles, LANES), f32),
-            pltpu.VMEM((plan.nx + 2, cells_y * plan.rows, LANES), f32),
-            pltpu.VMEM((plan.nx, cells_y * plan.rows, LANES), f32),
-            pltpu.VMEM((plan.nx, 3, cells_y * plan.rows, LANES), f32),
-            pltpu.VMEM((plan.nx, 3, cells_y * plan.rows, LANES), f32),
-            pltpu.VMEM((plan.nx, 4, plan.rows, LANES), f32),
-            pltpu.VMEM((3, cells_y * plan.rows, LANES), f32),
-            pltpu.VMEM((edges, 3, cells_y, LANES), f32),
-            pltpu.VMEM((2, 3, cells_y, LANES), f32),
+            pltpu.VMEM((plan.win_tiles, cells_y, LANES), f32),
+            pltpu.VMEM((plan.nx, 3, plan.win_tiles, cells_y, LANES), f32),
+            pltpu.VMEM((plan.nx, 3, plan.rows, cells_y, LANES), f32),
+            pltpu.VMEM((plan.nx, 4, plan.rows * 8, LANES), f32),
+            pltpu.VMEM((3, plan.rows * 8, LANES), f32),
+            pltpu.VMEM((3, plan.win_tiles, cells_y, LANES), f32),
             pltpu.VMEM((plan.nx, plan.groups, 4 * n, LANES), f32),
             pltpu.VMEM((views, 4 * n, LANES), f32),
             dma((plan.nx,)),

time: 17.9 us -> 17.6 us (0.983)
  the two profiles are of different devices: /device:TPU:31 before, /device:TPU:0 now
where the time goes in v4:
time: 17.6 us; the launch traced here: 17.4 us
  Pallas kernels  15.5 us (88%)
  local copies, waits for them, and re-layouts  1.3 us (7%)
  between operations  0.66 us (4%)
    pallas_call x1, Pallas kernels, body(): pl.pallas_call(functools.partial(kernel, plan), out_shape=jax.ShapeDtypeS...  15.5 us
    unnamed x1, local copies, waits for them, and re-layouts  1.3 us

profile of v4, /device:TPU:0, one launch (start us, length us, event | category | flops | bytes accessed | tf_op | source)
XLA Modules:
  0.0 17.4 jit_solution(14033064232665916712)
XLA Ops:
  0.7 15.5 %shard_map.64 = f32[4,512]{1,0:T(4,128)} custom-call(bf16[4,16,2048]{2,1,0:T(8,128)(2,1)} %density.1, s32[1,1,16]{2,1,0:T(1,128)} %occupied_hbm.1, f32[1,1]{1,0:T(1,128)} %bitcast.1.view_sign_hbm, f32[4,4]{1,0:T(4,128)} %transfer_hbm.1, f32[3]{0:T(128)} %absorb_hbm.1, f32[3,16,2048]{2,1,0:T(8,128)} %light_in.1), custom_call_target="tpu_custom_call" | custom-call | tf_op jit(solution)/shard_map/pallas_call | solution.py:394
  16.1 1.3 %copy.9 = f32[4,512]{1,0:T(4,128)} copy(f32[4,512]{1,0:T(4,128)} %shard_map.64) | data formatting | bytes 16384

commit v5 on v4

--- a/solution.py
+++ b/solution.py
@@ -43,10 +43,10 @@
     absorb_hbm,
     light_in,
     out,
-    occupied,
     view_sign,
     transfer,
     absorb,
+    bricks,
     wbuf,
     lbuf,
     occ,
@@ -77,7 +77,6 @@
         pltpu.make_async_copy(src, dst, lsem.at[i])
         for i, (src, dst) in enumerate(
             (
-                (occupied_hbm, occupied),
                 (view_sign_hbm, view_sign),
                 (transfer_hbm, transfer),
                 (absorb_hbm, absorb),
@@ -115,11 +114,7 @@
     light_copy = pltpu.make_async_copy(light_in.at[:, :, columns_of(me_l)], lbuf, lsem.at[4])
     light_copy.start()
 
-    for copy in small_copies:
-        copy.wait()
-    for k in range(plan.bricks):
-        value = jnp.full((plan.tiles_per_brick, LANES), occupied[0, 0, k].astype(jnp.float32))
-        occ[me_l, k * plan.tiles_per_brick : (k + 1) * plan.tiles_per_brick, :] = value
+    pltpu.make_async_copy(occupied_hbm.at[0], bricks.at[me_l], osem.at[me_l]).start()
 
     @pl.when(slab_of_me == me_l)
     def _():
@@ -131,8 +126,8 @@
 
     def occ_copy(k):
         return pltpu.make_async_remote_copy(
-            src_ref=occ.at[me_l],
-            dst_ref=occ.at[me_l],
+            src_ref=occupied_hbm.at[0],
+            dst_ref=bricks.at[me_l],
             send_sem=osend.at[k],
             recv_sem=osem.at[me_l],
             device_id={"light": (me_l + k) % lights, "view": me_v},
@@ -156,6 +151,9 @@
     for i in range(plan.cx):
         for k in range(1, lights):
             dens_copy(k, i).start()
+
+    for copy in small_copies:
+        copy.wait()
 
     tile_shape = (cy, LANES)
     lane = lax.broadcasted_iota(jnp.int32, tile_shape, 1)
@@ -197,10 +195,15 @@
     def wait_layer(x):
         pltpu.make_async_copy(wbuf.at[x + 1], wbuf.at[x + 1], dsem.at[x]).wait()
 
+    tile_of = lax.broadcasted_iota(jnp.int32, (plan.tiles, plan.bricks), 0)
+    brick_of = lax.broadcasted_iota(jnp.int32, (plan.tiles, plan.bricks), 1)
+    own_brick = tile_of // plan.tiles_per_brick == brick_of
+
     def wait_occ(block):
-        @pl.when(block != me_l)
-        def _():
-            pltpu.make_async_copy(occ.at[block], occ.at[block], osem.at[block]).wait()
+        pltpu.make_async_copy(bricks.at[block], bricks.at[block], osem.at[block]).wait()
+        row = jnp.broadcast_to(bricks[block], own_brick.shape).astype(jnp.float32)
+        held = jnp.sum(jnp.where(own_brick, row, 0.0), axis=1, keepdims=True)
+        occ[block] = jnp.broadcast_to(held, (plan.tiles, LANES))
 
     def prepare(x):
         block = x // plan.cx
@@ -309,6 +312,7 @@
         wait_layer(start - 1)
 
     wait_layer(start)
+    wait_occ(me_l)
 
     def arrive(x):
         new = jnp.logical_and(x < plan.nx, jnp.logical_and(x != start, x != start - 1))
@@ -317,7 +321,7 @@
         def _():
             wait_layer(x)
 
-        @pl.when(jnp.logical_and(new, x % plan.cx == 0))
+        @pl.when(jnp.logical_and(new, jnp.logical_and(x % plan.cx == 0, x // plan.cx != me_l)))
         def _():
             wait_occ(x // plan.cx)
 
@@ -397,10 +401,10 @@
         in_specs=[hbm] * 6,
         out_specs=pl.BlockSpec(memory_space=pltpu.VMEM),
         scratch_shapes=[
-            pltpu.SMEM(occupied.shape, occupied.dtype),
             pltpu.SMEM((1, 1), f32),
             pltpu.SMEM(transfer.shape, f32),
             pltpu.SMEM(absorb.shape, f32),
+            pltpu.VMEM((lights,) + occupied.shape[1:], occupied.dtype),
             pltpu.VMEM((plan.nx + 2, cells_y, plan.width), density.dtype),
             pltpu.VMEM((3, cells_y, plan.width), f32),
             pltpu.VMEM((lights, plan.tiles, LANES), f32),

time: 17.6 us -> 17.5 us (level)
  Pallas kernels: 15.5 us -> 15.3 us
where the time goes in v5:
time: 17.5 us; the launch traced here: 17.3 us
  Pallas kernels  15.3 us (87%)
  local copies, waits for them, and re-layouts  1.3 us (7%)
  between operations  0.66 us (4%)
    pallas_call x1, Pallas kernels, body(): pl.pallas_call(functools.partial(kernel, plan), out_shape=jax.ShapeDtypeS...  15.3 us
    unnamed x1, local copies, waits for them, and re-layouts  1.3 us

profile of v5, /device:TPU:0, one launch (start us, length us, event | category | flops | bytes accessed | tf_op | source)
XLA Modules:
  0.0 17.3 jit_solution(17279210997630721073)
XLA Ops:
  0.7 15.3 %shard_map.64 = f32[4,512]{1,0:T(4,128)} custom-call(bf16[4,16,2048]{2,1,0:T(8,128)(2,1)} %density.1, s32[1,1,16]{2,1,0:T(1,128)} %occupied_hbm.1, f32[1,1]{1,0:T(1,128)} %bitcast.1.view_sign_hbm, f32[4,4]{1,0:T(4,128)} %transfer_hbm.1, f32[3]{0:T(128)} %absorb_hbm.1, f32[3,16,2048]{2,1,0:T(8,128)} %light_in.1), custom_call_target="tpu_custom_call" | custom-call | tf_op jit(solution)/shard_map/pallas_call | solution.py:398
  16.0 1.3 %copy.9 = f32[4,512]{1,0:T(4,128)} copy(f32[4,512]{1,0:T(4,128)} %shard_map.64) | data formatting | bytes 16384

commit v6 on v5

--- a/solution.py
+++ b/solution.py
@@ -50,7 +50,6 @@
     wbuf,
     lbuf,
     occ,
-    exts,
     transmit,
     lit,
     base,
@@ -184,6 +183,14 @@
     wbuf[0] = blank
     wbuf[plan.nx + 1] = blank
 
+    places = [off + t for t in range(rows)]
+    if lights == 2:
+        places += [jnp.where(me_l == 0, rows, 0)]
+        halo_masks = [jnp.where(last_lane, has_left, jnp.where(first_lane, has_right, 1.0))]
+    else:
+        places += [jnp.minimum(off + rows, plan.win_tiles - 1), jnp.maximum(off - 1, 0)]
+        halo_masks = [has_right, has_left]
+
     def tile_at(ref, lead, t):
         return ref[lead, :, pl.ds(pl.multiple_of(t * LANES, LANES), LANES)].astype(jnp.float32)
 
@@ -207,14 +214,16 @@
 
     def prepare(x):
         block = x // plan.cx
-        for t in range(plan.win_tiles):
-            held = occ[block, pl.ds(win + t, 1), :]
-            cells = tile_at(wbuf, x + 1, t)
+        depths = []
+        for t, place in enumerate(places):
+            held = occ[block, pl.ds(win + place, 1), :]
+            cells = tile_at(wbuf, x + 1, place)
             ext = jnp.log(1.0 + jnp.exp(cubic(ext_coeffs, cells))) * held
-            exts[t] = ext
+            if t < rows:
+                depths.append(path_rate * ext)
             for c in range(3):
-                transmit[x, c, t] = jnp.exp(rates[c] * ext)
-        depths = [path_rate * exts[off + t] for t in range(rows)]
+                through = jnp.exp(rates[c] * ext)
+                transmit[x, c, t] = through if t < rows else through * halo_masks[t - rows]
         high = [depth.astype(jnp.bfloat16) for depth in depths]
         low = [
             (depth - h.astype(jnp.float32)).astype(jnp.bfloat16) for depth, h in zip(depths, high)
@@ -252,16 +261,16 @@
         pixels = []
         for c in range(3):
             for t in range(rows):
-                share = front[c, off + t] * lit[x, c, t]
+                share = front[c, t] * lit[x, c, t]
                 column[c, t * 8 : (t + 1) * 8, :] = base[x, c, t * 8 : (t + 1) * 8, :] + sum(
                     share[k : k + 8] for k in range(0, cy, 8)
                 )
             prods = [front[c, t] * transmit[x, c, t] for t in range(plan.win_tiles)]
-            outside = jnp.zeros(tile_shape, jnp.float32)
-            prods = [outside] + prods + [outside]
             for t in range(plan.win_tiles):
-                before, after = next_to(prods[t], prods[t + 1], prods[t + 2])
-                front[c, t] = 0.5 * prods[t + 1] + 0.25 * (before + after)
+                before, after = next_to(
+                    prods[t - 1], prods[t], prods[(t + 1) % plan.win_tiles]
+                )
+                front[c, t] = 0.5 * prods[t] + 0.25 * (before + after)
         for c in range(3):
             pixels.append(sum(column[c, pl.ds(r, rows, stride=8), :] for r in range(8)))
         pixels.append(base[x, 3, pl.ds(0, rows, stride=8), :])
@@ -304,8 +313,8 @@
 
     light_copy.wait()
     for c in range(3):
-        for t in range(plan.win_tiles):
-            front[c, t] = lbuf[c, :, t * LANES : (t + 1) * LANES]
+        for t, place in enumerate(places):
+            front[c, t] = tile_at(lbuf, c, place)
 
     @pl.when(me_l > 0)
     def _():
@@ -397,7 +406,7 @@
     dma = pltpu.SemaphoreType.DMA
     return pl.pallas_call(
         functools.partial(kernel, plan),
-        out_shape=jax.ShapeDtypeStruct((4, n * LANES), f32),
+        out_shape=pltpu.VMEM((4, n * LANES), f32),
         in_specs=[hbm] * 6,
         out_specs=pl.BlockSpec(memory_space=pltpu.VMEM),
         scratch_shapes=[
@@ -408,7 +417,6 @@
             pltpu.VMEM((plan.nx + 2, cells_y, plan.width), density.dtype),
             pltpu.VMEM((3, cells_y, plan.width), f32),
             pltpu.VMEM((lights, plan.tiles, LANES), f32),
-            pltpu.VMEM((plan.win_tiles, cells_y, LANES), f32),
             pltpu.VMEM((plan.nx, 3, plan.win_tiles, cells_y, LANES), f32),
             pltpu.VMEM((plan.nx, 3, plan.rows, cells_y, LANES), f32),
             pltpu.VMEM((plan.nx, 4, plan.rows * 8, LANES), f32),
@@ -425,7 +433,7 @@
             dma((views,)),
         ],
         compiler_params=pltpu.CompilerParams(
-            collective_id=0, has_side_effects=True
+            collective_id=0, has_side_effects=True, vmem_limit_bytes=62 * 1024 * 1024
         ),
     )(density, occupied, view_sign.reshape(1, 1), transfer, absorb, light_in)
 

time: 17.5 us -> 16 us (0.914)
  Pallas kernels: 15.3 us -> 14.6 us
  local copies, waits for them, and re-layouts: 1.3 us -> 0.6 us
    pallas_call x1, Pallas kernels: 15.3 us -> 14.6 us  [body(): pl.pallas_call(functools.partial(kernel, plan), out_shape=pltpu.VMEM((4,...]
    unnamed x1, local copies, waits for them, and re-layouts: 1.3 us -> 0.6 us
where the time goes in v6:
time: 16 us; the launch traced here: 15.9 us
  Pallas kernels  14.6 us (91%)
  between operations  0.66 us (4%)
  local copies, waits for them, and re-layouts  0.6 us (4%)
    pallas_call x1, Pallas kernels, body(): pl.pallas_call(functools.partial(kernel, plan), out_shape=pltpu.VMEM((4,...  14.6 us
    unnamed x1, local copies, waits for them, and re-layouts  0.6 us

profile of v6, /device:TPU:0, one launch (start us, length us, event | category | flops | bytes accessed | tf_op | source)
XLA Modules:
  0.0 15.9 jit_solution(14507153849837389731)
XLA Ops:
  0.7 14.6 %shard_map.64 = f32[4,512]{1,0:T(4,128)S(1)} custom-call(bf16[4,16,2048]{2,1,0:T(8,128)(2,1)} %density.1, s32[1,1,16]{2,1,0:T(1,128)} %occupied_hbm.1, f32[1,1]{1,0:T(1,128)} %bitcast.1.view_sign_hbm, f32[4,4]{1,0:T(4,128)} %transfer_hbm.1, f32[3]{0:T(128)} %absorb_hbm.1, f32[3,16,2048]{2,1,0:T(8,128)} %light_in.1), custom_call_target="tpu_custom_call" | custom-call | tf_op jit(solution)/shard_map/pallas_call | solution.py:407
  15.3 0.6 %copy.8 = f32[4,512]{1,0:T(4,128)} copy(f32[4,512]{1,0:T(4,128)S(1)} %shard_map.64) | data formatting | bytes 16384

commit v7 on v6

--- a/solution.py
+++ b/solution.py
@@ -334,23 +334,25 @@
         def _():
             wait_occ(x // plan.cx)
 
+    def arrive_for(step):
+        x = (start + step) % plan.nx
+
+        @pl.when(jnp.logical_and(x == 0, step > 0))
+        def _():
+            arrive(0)
+
+        arrive(x + 1)
+        return x
+
     def early(step, carry):
-        x = start + step
-        arrive(x + 1)
+        prepare(arrive_for(step))
+        return carry
+
+    def both(step, carry):
+        x = arrive_for(step)
+        shine(x - 1)
         prepare(x)
-        return carry
-
-    def both(step, carry):
-        x = (start + step) % plan.nx
-
-        @pl.when(jnp.logical_and(x == 0, step > 0))
-        def _():
-            arrive(0)
-
-        arrive(x + 1)
-        prepare(x)
-        shine(x)
-        send_layer(x)
+        send_layer(x - 1)
         return carry
 
     def late(x, carry):
@@ -358,9 +360,9 @@
         send_layer(x)
         return carry
 
-    lax.fori_loop(0, lead, early, 0)
-    lax.fori_loop(lead, plan.nx, both, 0)
-    lax.fori_loop(plan.nx - lead, plan.nx, late, 0)
+    lax.fori_loop(0, lead + 1, early, 0)
+    lax.fori_loop(lead + 1, plan.nx, both, 0)
+    lax.fori_loop(plan.nx - 1 - lead, plan.nx, late, 0)
 
     n = plan.piece_rows
     small = (n, LANES)

time: 16 us -> 16.2 us (1.012)
  Pallas kernels: 14.6 us -> 14.8 us
where the time goes in v7:
time: 16.2 us; the launch traced here: 16 us
  Pallas kernels  14.8 us (91%)
  between operations  0.66 us (4%)
  local copies, waits for them, and re-layouts  0.6 us (4%)
    pallas_call x1, Pallas kernels, body(): pl.pallas_call(functools.partial(kernel, plan), out_shape=pltpu.VMEM((4,...  14.8 us
    unnamed x1, local copies, waits for them, and re-layouts  0.6 us

profile of v7, /device:TPU:0, one launch (start us, length us, event | category | flops | bytes accessed | tf_op | source)
XLA Modules:
  0.0 16.0 jit_solution(8443111348215053464)
XLA Ops:
  0.7 14.8 %shard_map.64 = f32[4,512]{1,0:T(4,128)S(1)} custom-call(bf16[4,16,2048]{2,1,0:T(8,128)(2,1)} %density.1, s32[1,1,16]{2,1,0:T(1,128)} %occupied_hbm.1, f32[1,1]{1,0:T(1,128)} %bitcast.1.view_sign_hbm, f32[4,4]{1,0:T(4,128)} %transfer_hbm.1, f32[3]{0:T(128)} %absorb_hbm.1, f32[3,16,2048]{2,1,0:T(8,128)} %light_in.1), custom_call_target="tpu_custom_call" | custom-call | tf_op jit(solution)/shard_map/pallas_call | solution.py:409
  15.4 0.6 %copy.8 = f32[4,512]{1,0:T(4,128)} copy(f32[4,512]{1,0:T(4,128)S(1)} %shard_map.64) | data formatting | bytes 16384

commit v8 on v6

--- a/solution.py
+++ b/solution.py
@@ -362,36 +362,39 @@
     lax.fori_loop(lead, plan.nx, both, 0)
     lax.fori_loop(plan.nx - lead, plan.nx, late, 0)
 
-    n = plan.piece_rows
-    small = (n, LANES)
-    back = jnp.full(small, view_sign[0, 0]) < 0.0
-
-    def merge(v, carry):
-        pltpu.make_async_copy(recv.at[v], recv.at[v], rsem.at[v]).wait()
-        through, acc = carry[0], carry[1:]
-        passing = 1.0 - recv[v, 3 * n : 4 * n, :]
-        weight = jnp.where(back, 1.0, through)
-        keep = jnp.where(back, passing, 1.0)
-        acc = [keep * acc[c] + weight * recv[v, c * n : (c + 1) * n, :] for c in range(3)]
-        return (through * passing, *acc)
-
-    zero = jnp.zeros(small, jnp.float32)
-    merged = lax.fori_loop(0, views, merge, (jnp.ones(small, jnp.float32), zero, zero, zero))
-    pixels = list(merged[1:]) + [1.0 - merged[0]]
-    for c in range(4):
-        for r in range(n):
-            out[c : c + 1, r * LANES : (r + 1) * LANES] = pixels[c][r : r + 1, :]
-
     def finish(x, carry):
         for j in range(plan.groups):
             send_piece(x, j, False)
         return carry
 
-    lax.fori_loop(0, plan.nx, finish, 0)
     for k in range(1, lights):
         occ_copy(k).wait_send()
         for i in range(plan.cx):
             dens_copy(k, i).wait_send()
+    lax.fori_loop(0, plan.nx, finish, 0)
+
+    n = plan.piece_rows
+    small = (n, LANES)
+    back = jnp.full(small, view_sign[0, 0]) < 0.0
+
+    def wait_piece(v, carry):
+        pltpu.make_async_copy(recv.at[v], recv.at[v], rsem.at[v]).wait()
+        return carry
+
+    lax.fori_loop(0, views, wait_piece, 0)
+    through = jnp.ones(small, jnp.float32)
+    acc = [jnp.zeros(small, jnp.float32) for _ in range(3)]
+    for v in range(views):
+        passing = 1.0 - recv[v, 3 * n : 4 * n, :]
+        weight = jnp.where(back, 1.0, through)
+        keep = jnp.where(back, passing, 1.0)
+        through = through * passing
+        for c in range(3):
+            acc[c] = keep * acc[c] + weight * recv[v, c * n : (c + 1) * n, :]
+    pixels = acc + [1.0 - through]
+    for c in range(4):
+        for r in range(n):
+            out[c : c + 1, r * LANES : (r + 1) * LANES] = pixels[c][r : r + 1, :]
 
 
 def body(density, occupied, view_sign, transfer, absorb, light_in):

time: 16 us -> 16.1 us (level)
  no operation moved by 1% of the time
where the time goes in v8:
time: 16.1 us; the launch traced here: 16 us
  Pallas kernels  14.7 us (91%)
  between operations  0.66 us (4%)
  local copies, waits for them, and re-layouts  0.6 us (4%)
    pallas_call x1, Pallas kernels, body(): pl.pallas_call(functools.partial(kernel, plan), out_shape=pltpu.VMEM((4,...  14.7 us
    unnamed x1, local copies, waits for them, and re-layouts  0.6 us

profile of v8, /device:TPU:0, one launch (start us, length us, event | category | flops | bytes accessed | tf_op | source)
XLA Modules:
  0.0 16.0 jit_solution(9829614721653022309)
XLA Ops:
  0.7 14.7 %shard_map.64 = f32[4,512]{1,0:T(4,128)S(1)} custom-call(bf16[4,16,2048]{2,1,0:T(8,128)(2,1)} %density.1, s32[1,1,16]{2,1,0:T(1,128)} %occupied_hbm.1, f32[1,1]{1,0:T(1,128)} %bitcast.1.view_sign_hbm, f32[4,4]{1,0:T(4,128)} %transfer_hbm.1, f32[3]{0:T(128)} %absorb_hbm.1, f32[3,16,2048]{2,1,0:T(8,128)} %light_in.1), custom_call_target="tpu_custom_call" | custom-call | tf_op jit(solution)/shard_map/pallas_call | solution.py:410
  15.4 0.6 %copy.8 = f32[4,512]{1,0:T(4,128)} copy(f32[4,512]{1,0:T(4,128)S(1)} %shard_map.64) | data formatting | bytes 16384

commit v9 on v6

--- a/solution.py
+++ b/solution.py
@@ -111,7 +111,6 @@
             density.at[i, :, columns_of(me_l)], wbuf.at[layer + 1], dsem.at[layer]
         ).start()
     light_copy = pltpu.make_async_copy(light_in.at[:, :, columns_of(me_l)], lbuf, lsem.at[4])
-    light_copy.start()
 
     pltpu.make_async_copy(occupied_hbm.at[0], bricks.at[me_l], osem.at[me_l]).start()
 
@@ -150,6 +149,7 @@
     for i in range(plan.cx):
         for k in range(1, lights):
             dens_copy(k, i).start()
+    light_copy.start()
 
     for copy in small_copies:
         copy.wait()
@@ -311,11 +311,6 @@
     start = jnp.where(me_l > 0, me_l * plan.cx + 1, 0)
     lead = jnp.where(me_l > 0, plan.nx - start, 0)
 
-    light_copy.wait()
-    for c in range(3):
-        for t, place in enumerate(places):
-            front[c, t] = tile_at(lbuf, c, place)
-
     @pl.when(me_l > 0)
     def _():
         wait_layer(start - 1)
@@ -359,6 +354,12 @@
         return carry
 
     lax.fori_loop(0, lead, early, 0)
+
+    light_copy.wait()
+    for c in range(3):
+        for t, place in enumerate(places):
+            front[c, t] = tile_at(lbuf, c, place)
+
     lax.fori_loop(lead, plan.nx, both, 0)
     lax.fori_loop(plan.nx - lead, plan.nx, late, 0)
 

time: 16 us -> 16 us (level)
  no operation moved by 1% of the time
where the time goes in v9:
time: 16 us; the launch traced here: 15.9 us
  Pallas kernels  14.6 us (91%)
  between operations  0.66 us (4%)
  local copies, waits for them, and re-layouts  0.6 us (4%)
    pallas_call x1, Pallas kernels, body(): pl.pallas_call(functools.partial(kernel, plan), out_shape=pltpu.VMEM((4,...  14.6 us
    unnamed x1, local copies, waits for them, and re-layouts  0.6 us

profile of v9, /device:TPU:0, one launch (start us, length us, event | category | flops | bytes accessed | tf_op | source)
XLA Modules:
  0.0 15.9 jit_solution(13302479644598672050)
XLA Ops:
  0.7 14.6 %shard_map.64 = f32[4,512]{1,0:T(4,128)S(1)} custom-call(bf16[4,16,2048]{2,1,0:T(8,128)(2,1)} %density.1, s32[1,1,16]{2,1,0:T(1,128)} %occupied_hbm.1, f32[1,1]{1,0:T(1,128)} %bitcast.1.view_sign_hbm, f32[4,4]{1,0:T(4,128)} %transfer_hbm.1, f32[3]{0:T(128)} %absorb_hbm.1, f32[3,16,2048]{2,1,0:T(8,128)} %light_in.1), custom_call_target="tpu_custom_call" | custom-call | tf_op jit(solution)/shard_map/pallas_call | solution.py:408
  15.3 0.6 %copy.8 = f32[4,512]{1,0:T(4,128)} copy(f32[4,512]{1,0:T(4,128)S(1)} %shard_map.64) | data formatting | bytes 16384
